TPU v7x, 256 devices: a whole 4x4x8 slice. The times are simulated.
256 devices in a mesh: leaf: 8 (over y, core), front: 32 (over z, x).
Axes of the slice: x: 4, y: 4, z: 8, core: 2. Of those that a mesh axis runs over, the one named last changes fastest.
Arguments:
- leaf_inverse: bfloat16 [8192, 128, 128], P(('leaf', 'front')), may hold values from -0.5 to 0.5
- leaf_rhs: bfloat16 [8192, 128, 256], P(('leaf', 'front')), may hold values from -6 to 6
- off_blocks: bfloat16 [8192, 5, 128, 128], P(('leaf', 'front')), may hold values from -0.0546875 to 0.0546875
- block_rows: int32 [8192, 5], P(('leaf', 'front')), may hold values from 0 to 63
- fill_count: int32 [8192], P(('leaf', 'front')), may hold values from 1 to 5
- sep_rhs: bfloat16 [256, 128, 256], P(('leaf', 'front')), may hold values from -6 to 6
- panel_order: int32 [8, 32], P('leaf'), may hold values from 0 to 31, each once within a row
- sep_inverse: bfloat16 [256, 128, 4096], P(('leaf', 'front')), may hold values from -0.09375 to 0.09375
Outputs:
- leaf_solution: bfloat16 [8192, 128, 256], P(('leaf', 'front'))
- sep_forward: bfloat16 [256, 128, 256], P(('leaf', 'front'))
- sep_solution: float32 [256, 128, 256], P(('leaf', 'front'))
Inputs may be any that keep to these rules, and one draw needn't show every extreme that they name: Each row of panel_order is a permutation of the 32 separators of that front.
All inputs are finite; a program needn't handle non-finite values.
Results may differ from a plain program's by a relative error of at most 0.025.
Values may be sent and summed in bfloat16 or wider, within the bound.
No kernel may reach another device: no remote copies, remote signals or barrier semaphores. Data moves between devices by JAX's collectives and lax.ppermute only.
A program may use at most 128 MiB of HBM per device.

v0:
```python
import jax
import jax.numpy as jnp
from jax import lax
from jax.sharding import PartitionSpec as P


def swapped(shard, axis, bit):
    return lax.ppermute(shard, axis, [(i, i ^ 1 << bit) for i in range(lax.axis_size(axis))])


def on_device(
    leaf_inverse, leaf_rhs, off_blocks, block_rows, fill_count, sep_rhs, panel_order, sep_inverse
):
    block_width = leaf_inverse.shape[1]
    probe_count = leaf_rhs.shape[2]
    owned_count = sep_rhs.shape[0]
    fronts = lax.axis_size("front")
    front_seps = owned_count * fronts
    parity = lax.axis_index("leaf") % 2
    forward = jnp.einsum(
        "kab,kbr->kar", leaf_inverse, leaf_rhs, preferred_element_type=jnp.float32
    ).astype(jnp.bfloat16)
    used_slots = jnp.arange(off_blocks.shape[1], dtype=jnp.int32)[None, :] < fill_count[:, None]
    product = jnp.einsum("kpab,kbr->kpar", off_blocks, forward, preferred_element_type=jnp.float32)
    product = jnp.where(used_slots[:, :, None, None], product, jnp.zeros((), jnp.float32))
    product = product.reshape(-1, block_width, probe_count)
    half_index = block_rows // front_seps
    local_index = block_rows % front_seps
    sibling_flag = (half_index != parity).astype(jnp.int32)
    target = (
        local_index // owned_count * (2 * owned_count)
        + sibling_flag * owned_count
        + local_index % owned_count
    )
    partial_terms = (
        jnp.zeros((2 * front_seps, block_width, probe_count), jnp.float32)
        .at[target.reshape(-1)]
        .add(product)
    )
    shares = lax.psum_scatter(
        partial_terms.astype(jnp.bfloat16), "front", scatter_dimension=0, tiled=True
    ).astype(jnp.float32)
    received = swapped(shares[owned_count:].astype(jnp.bfloat16), "leaf", 0).astype(jnp.float32)
    summed = shares[:owned_count] + received
    separator_in = (sep_rhs.astype(jnp.float32) - summed).astype(jnp.bfloat16)
    arrived = lax.all_gather(separator_in, "front", axis=0, tiled=True)
    arrived_rows = arrived.shape[0]
    columns = sep_inverse
    flat = arrived.reshape(arrived_rows * block_width, probe_count)
    forward_sep = jnp.einsum(
        "sac,cr->sar", columns, flat, preferred_element_type=jnp.float32
    ).astype(jnp.bfloat16)
    owned_rows = lax.dynamic_slice_in_dim(
        panel_order[0], lax.axis_index("front") * owned_count, owned_count
    )
    placed = (
        jnp.zeros((front_seps, block_width, probe_count), jnp.float32)
        .at[owned_rows]
        .set(forward_sep.astype(jnp.float32))
    )
    sep_forward = lax.psum_scatter(
        placed.astype(jnp.bfloat16), "front", scatter_dimension=0, tiled=True
    )
    columns = sep_inverse
    result = jnp.einsum("sac,sar->cr", columns, forward_sep, preferred_element_type=jnp.float32)
    sep_solution = lax.psum_scatter(
        result.reshape(owned_count * lax.axis_size("front"), block_width, probe_count).astype(
            jnp.bfloat16
        ),
        "front",
        scatter_dimension=0,
        tiled=True,
    ).astype(jnp.float32)
    solved = sep_solution.astype(jnp.bfloat16)
    whole_front = lax.all_gather(solved, "front", axis=0, tiled=True)
    other_front = swapped(whole_front, "leaf", 0)
    lower_front = jnp.where(parity == 0, whole_front, other_front)
    upper_front = jnp.where(parity == 0, other_front, whole_front)
    pair_field = jnp.concatenate([lower_front, upper_front], axis=0)
    picked = pair_field[block_rows]
    picked = jnp.where(used_slots[:, :, None, None], picked, jnp.zeros((), jnp.bfloat16))
    pulled = jnp.einsum("kpab,kpar->kbr", off_blocks, picked, preferred_element_type=jnp.float32)
    backward = (forward.astype(jnp.float32) - pulled).astype(jnp.bfloat16)
    leaf_solution = jnp.einsum(
        "kba,kbr->kar", leaf_inverse, backward, preferred_element_type=jnp.float32
    ).astype(jnp.bfloat16)
    return (leaf_solution, sep_forward, sep_solution)


def solution(mesh):
    placed = (
        P(("leaf", "front"), None, None),
        P(("leaf", "front"), None, None),
        P(("leaf", "front"), None, None, None),
        P(("leaf", "front"), None),
        P(("leaf", "front")),
        P(("leaf", "front"), None, None),
        P("leaf", None),
        P(("leaf", "front"), None, None),
    )
    return jax.shard_map(
        on_device,
        mesh=mesh,
        in_specs=placed,
        out_specs=(
            P(("leaf", "front"), None, None),
            P(("leaf", "front"), None, None),
            P(("leaf", "front"), None, None),
        ),
        check_vma=False,
    )
```

profile of v0, /device:TPU:8, one launch (start us, length us, event | category | flops | bytes accessed | tf_op | source)
XLA Modules:
  0.0 925.4 jit_solution(462579910879347742)
XLA Ops:
  7.2 0.0 copy-start
  7.2 0.0 reduce-scatter.4.cloned.1.call-start
  7.2 0.8 add_select_fusion
  8.1 0.1 copy.27
  8.2 0.1 reshape.113
  8.3 0.0 copy-start.4
  8.3 0.9 iota_compare_fusion
  9.2 0.0 copy-done
  9.2 2.1 convolution_convert_fusion
  11.3 0.0 copy-done.4
  11.3 0.0 copy-start.3
  11.3 9.0 broadcast_select_fusion
  20.3 0.0 copy-done.3
  20.3 21.2 %copy.29 = f32[160,128,256]{2,1,0:T(8,128)} copy(f32[160,128,256]{1,2,0:T(8,128)} %bitcast.45) | data formatting | bytes 41943040 | tf_op jit(solution)/shard_map/reshape | solution.py:26
  41.5 4.3 broadcast_in_dim.40
  45.8 48.1 %scatter_fusion = f32[64,128,256]{2,1,0:T(8,128)} fusion(f32[64,128,256]{2,1,0:T(8,128)} %broadcast_in_dim.40, s32[160]{0:T(256)S(1)} %bitcast.50, f32[160,128,256]{2,1,0:T(8,128)} %copy.29), kind=kCustom, calls=%fused_computation.1 | custom fusion | flops 5242880 | bytes 62915200 | tf_op jit(solution)/shard_map/scatter-add | solution.py:38
  93.9 6.0 convert_element_type.59
  99.8 0.0 reduce-scatter.4.cloned.1.call-update
  99.8 0.0 all-gather.3.cloned.1.call-start
  99.9 224.0 %reduce-scatter.4.cloned.1.call-done = bf16[2,128,256]{2,1,0:T(8,128)(2,1)} async-done(((bf16[64,128,256]{2,1,0:T(8,128)(2,1)}), bf16[2,128,256]{2,1,0:T(8,128)(2,1)}) %reduce-scatter.4.cloned.1.call-update) | async-done | bytes 131088 | tf_op jit(solution)/shard_map/reduce_scatter | solution.py:40
  323.9 0.8 slice.35
  324.7 0.0 collective-permute-start
  324.7 1.3 collective-permute-done
  326.0 0.0 copy-done.8
  326.0 1.5 subtract_convert_fusion
  327.5 0.0 all-gather.3.cloned.1.call-update
  327.5 0.0 reduce-scatter.6.cloned.1.call-start
  327.6 0.0 copy-done.5
  327.6 0.7 copy.44
  328.3 75.5 %all-gather.3.cloned.1.call-done = bf16[32,128,256]{2,1,0:T(8,128)(2,1)} async-done(((bf16[1,128,256]{2,1,0:T(8,128)(2,1)}), bf16[32,128,256]{2,1,0:T(8,128)(2,1)}) %all-gather.3.cloned.1.call-update) | async-done | bytes 2097168 | tf_op jit(solution)/shard_map/all_gather | solution.py:46
  403.8 2.4 convolution_convert_fusion.1
  406.1 2.0 convert_bitcast_fusion.1
  408.2 0.0 reduce-scatter.6.cloned.1.call-update
  408.2 0.0 all-gather.5.cloned.1.call-start
  408.2 213.6 %reduce-scatter.6.cloned.1.call-done = bf16[1,128,256]{1,2,0:T(8,128)(2,1)} async-done(((bf16[32,128,256]{1,2,0:T(8,128)(2,1)}), bf16[1,128,256]{1,2,0:T(8,128)(2,1)}) %reduce-scatter.6.cloned.1.call-update) | async-done | bytes 65552 | tf_op jit(solution)/shard_map/reduce_scatter | solution.py:66
  621.8 1.6 copy.31
  623.5 0.0 all-gather.5.cloned.1.call-update
  623.5 0.0 reduce-scatter.8.cloned.1.call-start
  623.5 0.0 copy-done.10
  623.6 0.6 constant_dynamic-slice_fusion
  626.1 0.0 copy-done.9
  626.1 0.7 and_reduce_fusion
  626.8 0.6 select_bitcast_fusion
  627.4 0.1 copy.36
  627.5 0.2 broadcast_in_dim.45
  627.7 0.0 copy-start.2
  627.8 1.3 copy-done.2
  629.1 0.0 reduce-scatter.8.cloned.1.call-update
  629.1 72.0 %all-gather.5.cloned.1.call-done = bf16[32,128,256]{2,1,0:T(8,128)(2,1)} async-done(((bf16[1,128,256]{2,1,0:T(8,128)(2,1)}), bf16[32,128,256]{2,1,0:T(8,128)(2,1)}) %all-gather.5.cloned.1.call-update) | async-done | bytes 2097168 | tf_op jit(solution)/shard_map/all_gather | solution.py:75
  701.1 0.0 collective-permute-start.1
  701.1 0.1 copy.32
  701.2 0.1 reshape.121
  701.3 0.0 copy-done.7
  701.3 0.8 copy.38
  702.1 3.5 collective-permute-done.1
  705.6 2.5 broadcast_select_fusion.2
  708.1 2.4 pad_maximum_fusion
  710.5 9.8 %gather_fusion = bf16[160,128,256]{2,1,0:T(8,128)(2,1)} fusion(bf16[64,128,256]{2,1,0:T(8,128)(2,1)} %pad_maximum_fusion, s32[1024]{0:T(1024)S(1)} %pad_clamp_fusion), kind=kCustom, calls=%fused_computation | custom fusion | bytes 20972160 | tf_op jit(solution)/shard_map/gather | solution.py:80
  720.3 15.1 %copy.33 = bf16[32,5,128,256]{2,3,1,0:T(8,128)(2,1)} copy(bf16[32,5,128,256]{3,2,1,0:T(8,128)(2,1)} %bitcast.46) | data formatting | bytes 20971520 | tf_op jit(solution)/shard_map/gather | solution.py:80
  735.4 0.0 copy-done.6
  735.4 9.2 convert_bitcast_fusion
  744.6 4.1 copy.37
  748.7 170.1 %reduce-scatter.8.cloned.1.call-done = bf16[1,128,256]{2,1,0:T(8,128)(2,1)} async-done(((bf16[32,128,256]{2,1,0:T(8,128)(2,1)}), bf16[1,128,256]{2,1,0:T(8,128)(2,1)}) %reduce-scatter.8.cloned.1.call-update) | async-done | bytes 65552 | tf_op jit(solution)/shard_map/reduce_scatter | solution.py:61
  918.9 0.0 copy-done.1
  (10 shorter events, 0.0 us)
Async XLA Ops:
  7.2 2.0 copy-start
  7.2 316.7 %reduce-scatter.4.cloned.1.call-start = ((), (), s32[]{:S(2)}) async-start(), calls=%async_computation.3 | async-start | bytes 4325376 | tf_op jit(solution)/shard_map/reduce_scatter | solution.py:40
  8.3 3.0 copy-start.4
  11.3 9.0 copy-start.3
  99.8 226.2 %copy-start.8 = (bf16[1,128,256]{2,1,0:T(8,128)(2,1)S(1)}, bf16[1,128,256]{2,1,0:T(8,128)(2,1)}, u32[]{:S(2)}) copy-start(bf16[1,128,256]{2,1,0:T(8,128)(2,1)} %param.15) | copy-start | bytes 196612
  99.8 227.8 %copy-start.5 = (bf16[1,128,4096]{2,1,0:T(8,128)(2,1)S(1)}, bf16[1,128,4096]{2,1,0:T(8,128)(2,1)}, u32[]{:S(2)}) copy-start(bf16[1,128,4096]{2,1,0:T(8,128)(2,1)} %param.17) | copy-start | bytes 3145732
  99.8 303.9 %all-gather.3.cloned.1.call-start = ((), (), s32[]{:S(2)}) async-start(), calls=%async_computation.4 | async-start | bytes 2162688 | tf_op jit(solution)/shard_map/all_gather | solution.py:46
  324.7 1.3 collective-permute-start
  327.5 294.3 %reduce-scatter.6.cloned.1.call-start = ((), (), s32[]{:S(2)}) async-start(), calls=%async_computation.5 | async-start | bytes 2162688 | tf_op jit(solution)/shard_map/reduce_scatter | solution.py:66
  403.7 219.8 %copy-start.10 = (s32[1,32]{1,0:T(1,128)S(1)}, s32[1,32]{1,0:T(1,128)}, u32[]{:S(2)}) copy-start(s32[1,32]{1,0:T(1,128)} %param.16) | copy-start | bytes 388
  403.8 222.3 %copy-start.9 = (s32[3]{0:T(128)S(1)}, s32[3]{0:T(128)}, u32[]{:S(2)}) copy-start(s32[3]{0:T(128)} %constant.102.clone.1) | copy-start | bytes 40
  408.2 292.9 %all-gather.5.cloned.1.call-start = ((), (), s32[]{:S(2)}) async-start(), calls=%async_computation.6 | async-start | bytes 2162688 | tf_op jit(solution)/shard_map/all_gather | solution.py:75
  621.8 79.5 %copy-start.7 = (bf16[1,128,256]{1,2,0:T(8,128)(2,1)S(1)}, bf16[1,128,256]{1,2,0:T(8,128)(2,1)}, u32[]{:S(2)}) copy-start(bf16[1,128,256]{1,2,0:T(8,128)(2,1)} %reduce-scatter.6.cloned.1.call-done) | copy-start | bytes 196612
  623.5 295.4 %reduce-scatter.8.cloned.1.call-start = ((), (), s32[]{:S(2)}) async-start(), calls=%async_computation.7 | async-start | bytes 2162688 | tf_op jit(solution)/shard_map/reduce_scatter | solution.py:61
  627.7 1.3 copy-start.2
  701.1 4.5 collective-permute-start.1
  720.3 15.1 %copy-start.6 = (bf16[32,128,128]{2,1,0:T(8,128)(2,1)S(1)}, bf16[32,128,128]{2,1,0:T(8,128)(2,1)}, u32[]{:S(2)}) copy-start(bf16[32,128,128]{2,1,0:T(8,128)(2,1)} %param.10) | copy-start | bytes 3145732
  735.4 183.4 %copy-start.1 = (bf16[32,128,256]{2,1,0:T(8,128)(2,1)S(1)}, bf16[32,128,256]{2,1,0:T(8,128)(2,1)}, u32[]{:S(2)}) copy-start(bf16[32,128,256]{2,1,0:T(8,128)(2,1)} %param.11) | copy-start | bytes 6291460
Sparse Core Ops, SparseCore 0:
  100.0 223.8 reduce-scatter.3
  327.6 76.0 all-gather.2
  408.3 213.4 reduce-scatter.5
  624.8 76.2 all-gather.4
  705.3 213.4 reduce-scatter.7
where the time goes:
time: 927 us; the launch traced here: 925 us
  waiting for transfers between devices  760 us (82%)
  other arithmetic  63.4 us (7%)
  local copies, waits for them, and re-layouts  61.1 us (7%)
  matrix products  24.7 us (3%)
  between operations  15.9 us (2%)
    reduce_scatter x1, waiting for transfers between devices, on_device(): lax.psum_scatter(partial_terms.astype(jnp.bfloat16), 'front', scatter_dim...  224 us
    reduce_scatter x1, waiting for transfers between devices, on_device(): lax.psum_scatter(result.reshape(owned_count * lax.axis_size('front'), blo...  214 us
    reduce_scatter x1, waiting for transfers between devices, on_device(): lax.psum_scatter(placed.astype(jnp.bfloat16), 'front', scatter_dimension=...  170 us
    all_gather x1, waiting for transfers between devices, on_device(): arrived = lax.all_gather(separator_in, 'front', axis=0, tiled=True)  75.5 us
    all_gather x1, waiting for transfers between devices, on_device(): whole_front = lax.all_gather(solved, 'front', axis=0, tiled=True)  72 us
    scatter-add x1, other arithmetic, on_device(): partial_terms = jnp.zeros((2 * front_seps, block_width, probe_count), jnp...  48.1 us
    gather x2, local copies, waits for them, and re-layouts, on_device(): picked = pair_field[block_rows]  24.9 us
    reshape x1, local copies, waits for them, and re-layouts, on_device(): product = product.reshape(-1, block_width, probe_count)  21.2 us
  transfers between devices with their start and end apart: 7, of which 7 were waited for; matrix products, arithmetic and copies ran while one was open for 5% of the time, Pallas kernels for 0%

commit v1 on v0

v1 whole, which is shorter than its diff:
```python
import functools

import jax
import jax.numpy as jnp
from jax import lax
from jax.experimental import pallas as pl
from jax.experimental.pallas import tpu as pltpu
from jax.sharding import PartitionSpec as P

X = 4
F32 = jnp.float32
BF16 = jnp.bfloat16


def groups(fronts):
    rows = fronts // X
    along_x = [[z * X + x for x in range(X)] for z in range(rows)]
    along_z = [[z * X + x for z in range(rows)] for x in range(X)]
    return along_x, along_z


def exchange(value, where):
    return lax.all_to_all(value, "front", 0, 0, tiled=True, axis_index_groups=where)


def sibling(value):
    size = lax.axis_size("leaf")
    return lax.ppermute(value, "leaf", [(i, i ^ 1) for i in range(size)])


def place(row, parity, seps):
    rows = seps // X
    local = lax.rem(row, seps)
    half = row // seps
    own = lax.rem(local, X) * rows + local // X
    return jnp.where(half == parity, own, own + seps)


def forward_kernel(per, slots, seps, rows_ref, fill_ref, parity_ref, inv_ref, rhs_ref, off_ref,
                   fwd_ref, out_ref, acc):
    step = pl.program_id(0)
    parity = parity_ref[0]

    @pl.when(step == 0)
    def _():
        acc[...] = jnp.zeros_like(acc)

    for k in range(per):
        leaf = step * per + k
        fwd = jnp.dot(inv_ref[k], rhs_ref[k], preferred_element_type=F32).astype(BF16)
        fwd_ref[k] = fwd
        fill = fill_ref[leaf]
        for p in range(slots):
            product = jnp.dot(off_ref[k, p], fwd, preferred_element_type=F32)
            spot = place(rows_ref[leaf * slots + p], parity, seps)
            spot = jnp.where(p < fill, spot, 2 * seps)
            acc[spot] += product

    @pl.when(step == pl.num_programs(0) - 1)
    def _():
        def body(i, _):
            out_ref[i] = acc[i].astype(BF16)
            return 0
        lax.fori_loop(0, 2 * seps, body, 0)


def forward_leaves(block_rows, fill_count, parity, leaf_inverse, leaf_rhs, off_blocks, seps, per=4):
    leaves, b, r = leaf_rhs.shape
    slots = off_blocks.shape[1]
    grid_spec = pltpu.PrefetchScalarGridSpec(
        num_scalar_prefetch=3,
        grid=(leaves // per,),
        in_specs=[
            pl.BlockSpec((per, b, b), lambda i, *_: (i, 0, 0)),
            pl.BlockSpec((per, b, r), lambda i, *_: (i, 0, 0)),
            pl.BlockSpec((per, slots, b, b), lambda i, *_: (i, 0, 0, 0)),
        ],
        out_specs=[
            pl.BlockSpec((per, b, r), lambda i, *_: (i, 0, 0)),
            pl.BlockSpec((2 * seps, b, r), lambda i, *_: (0, 0, 0)),
        ],
        scratch_shapes=[pltpu.VMEM((2 * seps + 1, b, r), F32)],
    )
    return pl.pallas_call(
        functools.partial(forward_kernel, per, slots, seps),
        grid_spec=grid_spec,
        out_shape=[
            jax.ShapeDtypeStruct((leaves, b, r), BF16),
            jax.ShapeDtypeStruct((2 * seps, b, r), BF16),
        ],
        compiler_params=pltpu.CompilerParams(vmem_limit_bytes=40 << 20),
    )(block_rows.reshape(-1), fill_count, parity, leaf_inverse, leaf_rhs, off_blocks)


def backward_kernel(per, slots, seps, rows_ref, fill_ref, parity_ref, inv_ref, fwd_ref, off_ref,
                    own_ref, other_ref, out_ref, field):
    step = pl.program_id(0)
    parity = parity_ref[0]

    @pl.when(step == 0)
    def _():
        field[pl.ds(0, seps)] = own_ref[...]
        field[pl.ds(seps, seps)] = other_ref[...]
        field[2 * seps] = jnp.zeros(field.shape[1:], field.dtype)

    for k in range(per):
        leaf = step * per + k
        fill = fill_ref[leaf]
        total = fwd_ref[k].astype(F32)
        for p in range(slots):
            spot = place(rows_ref[leaf * slots + p], parity, seps)
            spot = jnp.where(p < fill, spot, 2 * seps)
            total -= lax.dot_general(off_ref[k, p], field[spot], (((0,), (0,)), ((), ())),
                                     preferred_element_type=F32)
        out_ref[k] = lax.dot_general(inv_ref[k], total.astype(BF16), (((0,), (0,)), ((), ())),
                                     preferred_element_type=F32).astype(BF16)


def backward_leaves(block_rows, fill_count, parity, leaf_inverse, forward, off_blocks, own, other, per=4):
    leaves, b, r = forward.shape
    slots = off_blocks.shape[1]
    seps = own.shape[0]
    grid_spec = pltpu.PrefetchScalarGridSpec(
        num_scalar_prefetch=3,
        grid=(leaves // per,),
        in_specs=[
            pl.BlockSpec((per, b, b), lambda i, *_: (i, 0, 0)),
            pl.BlockSpec((per, b, r), lambda i, *_: (i, 0, 0)),
            pl.BlockSpec((per, slots, b, b), lambda i, *_: (i, 0, 0, 0)),
            pl.BlockSpec((seps, b, r), lambda i, *_: (0, 0, 0)),
            pl.BlockSpec((seps, b, r), lambda i, *_: (0, 0, 0)),
        ],
        out_specs=pl.BlockSpec((per, b, r), lambda i, *_: (i, 0, 0)),
        scratch_shapes=[pltpu.VMEM((2 * seps + 1, b, r), BF16)],
    )
    return pl.pallas_call(
        functools.partial(backward_kernel, per, slots, seps),
        grid_spec=grid_spec,
        out_shape=jax.ShapeDtypeStruct((leaves, b, r), BF16),
        compiler_params=pltpu.CompilerParams(vmem_limit_bytes=40 << 20),
    )(block_rows.reshape(-1), fill_count, parity, leaf_inverse, forward, off_blocks, own, other)


def on_device(
    leaf_inverse, leaf_rhs, off_blocks, block_rows, fill_count, sep_rhs, panel_order, sep_inverse
):
    b = leaf_inverse.shape[1]
    r = leaf_rhs.shape[2]
    seps = lax.axis_size("front")
    rows = seps // X
    along_x, along_z = groups(seps)
    parity = (lax.axis_index("leaf") % 2).astype(jnp.int32).reshape(1)
    me = lax.axis_index("front")
    my_x, my_z = me % X, me // X

    with jax.named_scope("spread_panels"):
        panels = sep_inverse.reshape(b, rows, X, b).transpose(2, 0, 1, 3).reshape(X, b, rows * b)
        panels = exchange(panels, along_x).reshape(X * b, rows * b)

    with jax.named_scope("leaf_forward"):
        forward, terms = forward_leaves(
            block_rows, fill_count, parity, leaf_inverse, leaf_rhs, off_blocks, seps
        )
    with jax.named_scope("sum_terms"):
        mine = terms[:seps].astype(F32) + sibling(terms[seps:]).astype(F32)
        got = exchange(mine.astype(BF16), along_x).reshape(X, rows, b, r)
        column = got.astype(F32).sum(0).astype(BF16)
        got = exchange(column, along_z)
        summed = got.astype(F32).sum(0)
    with jax.named_scope("separators"):
        separator_in = (sep_rhs[0].astype(F32) - summed).astype(BF16)
        right = exchange(jnp.broadcast_to(separator_in[None], (rows, b, r)), along_z)
        part = jnp.dot(panels, right.reshape(rows * b, r), preferred_element_type=F32).astype(BF16)
        parts = exchange(jnp.broadcast_to(part[None], (X, X * b, r)).reshape(X * X * b, r), along_x)
        solved_rows = parts.reshape(X, X * b, r).astype(F32).sum(0).astype(BF16)
        adjoint = lax.dot_general(panels, solved_rows, (((0,), (0,)), ((), ())), preferred_element_type=F32)
        got = exchange(adjoint.reshape(rows, b, r).astype(BF16), along_z)
        sep_solution = got.astype(F32).sum(0)
    with jax.named_scope("order_rows"):
        held = lax.dynamic_slice_in_dim(panel_order[0], my_z * X, X)
        wanted = jnp.arange(rows, dtype=jnp.int32) * X + my_x
        chosen = held[None, :] == wanted[:, None]
        blocks = jnp.where(
            chosen[:, :, None, None], solved_rows.reshape(1, X, b, r), jnp.zeros((), BF16)
        ).astype(F32).sum(1).astype(BF16)
        sep_forward = lax.psum_scatter(
            blocks, "front", scatter_dimension=0, tiled=True, axis_index_groups=along_z
        )
    with jax.named_scope("spread_solution"):
        solved = sep_solution.astype(BF16)
        column = exchange(jnp.broadcast_to(solved[None], (rows, b, r)), along_z)
        own = exchange(jnp.broadcast_to(column[None], (X, rows, b, r)).reshape(seps, b, r), along_x)
        other = sibling(own)
    with jax.named_scope("leaf_backward"):
        leaf_solution = backward_leaves(
            block_rows, fill_count, parity, leaf_inverse, forward, off_blocks, own, other
        )
    return leaf_solution, sep_forward, sep_solution[None]


def solution(mesh):
    both = ("leaf", "front")
    return jax.shard_map(
        on_device,
        mesh=mesh,
        in_specs=(
            P(both, None, None),
            P(both, None, None),
            P(both, None, None, None),
            P(both, None),
            P(both),
            P(both, None, None),
            P("leaf", None),
            P(both, None, None),
        ),
        out_specs=(P(both, None, None), P(both, None, None), P(both, None, None)),
        check_vma=False,
    )
```

time: 927 us -> 233 us (0.25)
  waiting for transfers between devices: 760 us -> 60.9 us
  blocking collectives: 0 us -> 98.7 us
  other arithmetic: 63.4 us -> 3.73 us
  local copies, waits for them, and re-layouts: 61.1 us -> 14.3 us
  Pallas kernels: 0 us -> 24.1 us
  matrix products: 24.7 us -> 0.94 us
  starting transfers between devices: 0.21 us -> 15.5 us
    reduce_scatter x3 -> x1, waiting for transfers between devices: 608 us -> 12.7 us  [on_device(): lax.psum_scatter(blocks, 'front', scatter_dimension=0, tiled=True, axis_i...]
    all_gather x2 -> x0, waiting for transfers between devices: 147 us -> none  [the longest x1 75.5 us: on_device(): arrived = lax.all_gather(separator_in, 'front', axis=0, tiled=True)]
    all_to_all x0 -> x5, blocking collectives: none -> 98.7 us  [exchange(): lax.all_to_all(value, 'front', 0, 0, tiled=True, axis_index_groups=where)]
    scatter-add x1 -> x0, other arithmetic: 48.1 us -> none  [on_device(): partial_terms = jnp.zeros((2 * front_seps, block_width, probe_count), jnp...]
    all_to_all x0 -> x3, waiting for transfers between devices: none -> 41.8 us  [exchange(): lax.all_to_all(value, 'front', 0, 0, tiled=True, axis_index_groups=where)]
    gather x2 -> x0, local copies, waits for them, and re-layouts: 24.9 us -> none  [on_device(): picked = pair_field[block_rows]]
    pallas_call x0 -> x2, Pallas kernels: none -> 24.1 us  [the longest x1 12.2 us: backward_leaves(): pl.pallas_call(functools.partial(backward_kernel, per, slots, seps), grid...]
    dot_general x5 -> x2, matrix products: 24.7 us -> 0.94 us  [the longest x1 0.49 us: on_device(): jnp.dot(panels, right.reshape(rows * b, r), preferred_element_type=F32)]
  transfers between devices with their start and end apart: 7 -> 6, of which waited for: 7 -> 6; matrix products, arithmetic and copies ran while one was open for 5% -> 2% of each run, Pallas kernels for 0% -> 5%
where the time goes in v1:
time: 233 us; the launch traced here: 232 us
  blocking collectives  98.7 us (42%)
  waiting for transfers between devices  60.9 us (26%)
  Pallas kernels  24.1 us (10%)
  starting transfers between devices  15.5 us (7%)
  local copies, waits for them, and re-layouts  14.3 us (6%)
  between operations  14.3 us (6%)
  other arithmetic  3.73 us (2%)
    all_to_all x5, blocking collectives, exchange(): lax.all_to_all(value, 'front', 0, 0, tiled=True, axis_index_groups=where)  98.7 us
    all_to_all x3, waiting for transfers between devices, exchange(): lax.all_to_all(value, 'front', 0, 0, tiled=True, axis_index_groups=where)  41.8 us
    all_to_all x3, starting transfers between devices, exchange(): lax.all_to_all(value, 'front', 0, 0, tiled=True, axis_index_groups=where)  15.5 us
    reduce_scatter x1, waiting for transfers between devices, on_device(): lax.psum_scatter(blocks, 'front', scatter_dimension=0, tiled=True, axis_i...  12.7 us
    pallas_call x1, Pallas kernels, backward_leaves(): pl.pallas_call(functools.partial(backward_kernel, per, slots, seps), grid...  12.2 us
    pallas_call x1, Pallas kernels, forward_leaves(): pl.pallas_call(functools.partial(forward_kernel, per, slots, seps), grid_...  11.9 us
    unnamed x25, local copies, waits for them, and re-layouts  10.9 us
    ppermute x2, waiting for transfers between devices, sibling(): return lax.ppermute(value, 'leaf', [(i, i ^ 1) for i in range(size)])  6.32 us
  transfers between devices with their start and end apart: 6, of which 6 were waited for; matrix products, arithmetic and copies ran while one was open for 2% of the time, Pallas kernels for 5%

profile of v1, /device:TPU:8, one launch (start us, length us, event | category | flops | bytes accessed | tf_op | source)
XLA Modules:
  0.0 232.5 jit_solution(17414418021738011290)
XLA Ops:
  7.2 0.0 copy-start
  7.2 0.8 copy.28
  8.0 0.1 reshape.82.rows_ref
  8.1 0.0 copy-start.2
  8.1 1.2 copy-done.2
  9.3 0.0 copy-start.4
  9.3 1.6 copy-done.4
  10.9 0.0 copy-start.7
  10.9 0.7 copy-done.7
  11.5 11.9 %leaf_forward.1 = (bf16[32,128,256]{2,1,0:T(8,128)(2,1)S(1)}, bf16[64,128,256]{2,1,0:T(8,128)(2,1)S(1)}) custom-call(s32[160]{0:T(256)S(1)} %reshape.82.rows_ref, s32[32]{0:T(128)S(1)} %copy-done.7, s32[1]{0:T(128)} %bitcast.parity_ref, bf16[32,128,128]{2,1,0:T(8,128)(2,1)S(1)} %copy-done.2, bf16[32,128,256]{2,1,0:T(8,128)(2,1)S(1)} %copy-done.4, ...), custom_call_target="tpu_custom_call" | custom-call | tf_op jit(solution)/shard_map/leaf_forward/pallas_call | solution.py:84
  23.5 0.0 copy-start.5
  23.5 0.1 slice.7
  23.6 1.2 copy-done.5
  24.8 0.0 collective-permute-start
  24.8 4.2 %collective-permute-done = bf16[32,128,256]{2,1,0:T(8,128)(2,1)S(1)} collective-permute-done((bf16[32,128,256]{2,1,0:T(8,128)(2,1)S(1)}, bf16[32,128,256]{2,1,0:T(8,128)(2,1)S(1)}, u32[]{:S(2)}, u32[]{:S(2)}) %collective-permute-start) | collective-permute-done | bytes 2097184 | tf_op jit(solution)/shard_map/sum_terms/ppermute | solution.py:28
  29.0 0.8 add_convert_fusion
  29.7 30.7 %all_to_all.41 = bf16[32,128,256]{2,1,0:T(8,128)(2,1)S(1)} all-to-all(bf16[32,128,256]{2,1,0:T(8,128)(2,1)S(1)} %add_convert_fusion), channel_id=1, replica_groups={{0,1,2,3},{4,5,6,7},{8,9,10,11},{12,13,14,15},{16,17,18,19},{20,21,22,2..., dimensions={0} | all-to-all | bytes 4194304 | tf_op jit(solution)/shard_map/sum_terms/all_to_all | solution.py:23
  60.5 0.0 copy-start.9
  60.5 1.3 reduce_sum.58
  61.7 8.5 %all-to-all-start.1 = ((bf16[8,128,256]{2,1,0:T(8,128)(2,1)}), bf16[8,128,256]{2,1,0:T(8,128)(2,1)S(1)}, u32[]{:S(2)}, u32[]{:S(2)}) async-start(bf16[8,128,256]{2,1,0:T(8,128)(2,1)} %reduce_sum.58), calls=%async_computation.1 | async-start | bytes 1048576 | tf_op jit(solution)/shard_map/sum_terms/all_to_all | solution.py:23
  70.2 0.0 copy-done.9
  70.2 0.7 copy.29
  70.9 0.0 copy-start.10
  70.9 1.0 copy.30
  71.9 14.6 %all-to-all-done.1 = bf16[8,128,256]{2,1,0:T(8,128)(2,1)S(1)} async-done(((bf16[8,128,256]{2,1,0:T(8,128)(2,1)}), bf16[8,128,256]{2,1,0:T(8,128)(2,1)S(1)}, u32[]{:S(2)}, u32[]{:S(2)}) %all-to-all-start.1) | async-done | bytes 524320 | tf_op jit(solution)/shard_map/sum_terms/all_to_all | solution.py:23
  86.6 3.5 %all-to-all-start.3 = ((bf16[4,128,1024]{1,2,0:T(8,128)(2,1)}), bf16[4,128,1024]{1,2,0:T(8,128)(2,1)S(1)}, u32[]{:S(2)}, u32[]{:S(2)}) async-start(bf16[4,128,1024]{1,2,0:T(8,128)(2,1)} %bitcast.7), calls=%async_computation.3 | async-start | bytes 2097152 | tf_op jit(solution)/shard_map/spread_panels/all_to_all | solution.py:23
  90.1 0.1 convert_reduce_fusion.1
  90.2 0.0 copy-done.10
  90.2 13.1 %all-to-all-done.3 = bf16[4,128,1024]{1,2,0:T(8,128)(2,1)S(1)} async-done(((bf16[4,128,1024]{1,2,0:T(8,128)(2,1)}), bf16[4,128,1024]{1,2,0:T(8,128)(2,1)S(1)}, u32[]{:S(2)}, u32[]{:S(2)}) %all-to-all-start.3) | async-done | bytes 1048608 | tf_op jit(solution)/shard_map/spread_panels/all_to_all | solution.py:23
  103.3 0.8 broadcast_in_dim.33
  104.1 3.5 %all-to-all-start.2 = ((bf16[8,128,256]{2,1,0:T(8,128)(2,1)}), bf16[8,128,256]{2,1,0:T(8,128)(2,1)S(1)}, u32[]{:S(2)}, u32[]{:S(2)}) async-start(bf16[8,128,256]{2,1,0:T(8,128)(2,1)} %broadcast_in_dim.33), calls=%async_computation.2 | async-start | bytes 1048576 | tf_op jit(solution)/shard_map/separators/all_to_all | solution.py:23
  107.6 0.0 reduce-scatter.2.cloned.1.call-start
  107.7 0.5 copy.31
  108.2 14.1 %all-to-all-done.2 = bf16[8,128,256]{2,1,0:T(8,128)(2,1)S(1)} async-done(((bf16[8,128,256]{2,1,0:T(8,128)(2,1)}), bf16[8,128,256]{2,1,0:T(8,128)(2,1)S(1)}, u32[]{:S(2)}, u32[]{:S(2)}) %all-to-all-start.2) | async-done | bytes 524320 | tf_op jit(solution)/shard_map/separators/all_to_all | solution.py:23
  122.3 0.5 fusion.1
  122.8 0.1 copy.32
  122.9 0.1 broadcast_in_dim.54
  123.0 14.0 %all_to_all.42 = bf16[4,512,256]{2,1,0:T(8,128)(2,1)S(1)} all-to-all(bf16[4,512,256]{2,1,0:T(8,128)(2,1)S(1)} %broadcast_in_dim.54), channel_id=1, replica_groups={{0,1,2,3},{4,5,6,7},{8,9,10,11},{12,13,14,15},{16,17,18,19},{20,21,22,2..., dimensions={0} | all-to-all | bytes 2097152 | tf_op jit(solution)/shard_map/separators/all_to_all | solution.py:23
  137.0 0.3 reduce_sum.61
  137.3 0.5 fusion
  137.7 0.1 copy.40
  137.8 15.7 %all_to_all.43 = bf16[8,128,256]{1,2,0:T(8,128)(2,1)S(1)} all-to-all(bf16[8,128,256]{1,2,0:T(8,128)(2,1)S(1)} %bitcast.40), channel_id=1, replica_groups={{0,4,8,12,16,20,24,28},{1,5,9,13,17,21,25,29},{2,6,10,14,18,22,26,30},{..., dimensions={0} | all-to-all | bytes 1048576 | tf_op jit(solution)/shard_map/separators/all_to_all | solution.py:23
  153.5 0.1 convert_reduce_fusion
  153.6 0.1 copy.35
  153.8 15.7 %all_to_all.44 = bf16[8,128,256]{2,1,0:T(8,128)(2,1)S(1)} all-to-all(bf16[8,128,256]{2,1,0:T(8,128)(2,1)S(1)} %broadcast_in_dim.55), channel_id=1, replica_groups={{0,4,8,12,16,20,24,28},{1,5,9,13,17,21,25,29},{2,6,10,14,18,22,26,30},{..., dimensions={0} | all-to-all | bytes 1048576 | tf_op jit(solution)/shard_map/spread_solution/all_to_all | solution.py:23
  169.5 0.2 broadcast_in_dim.56
  169.7 0.0 copy-start.3
  169.7 0.0 copy-start.8
  169.7 22.6 %all_to_all.45.own_ref = bf16[32,128,256]{2,1,0:T(8,128)(2,1)S(1)} all-to-all(bf16[32,128,256]{2,1,0:T(8,128)(2,1)S(1)} %bitcast.35), channel_id=1, replica_groups={{0,1,2,3},{4,5,6,7},{8,9,10,11},{12,13,14,15},{16,17,18,19},{20,21,22,2..., dimensions={0} | all-to-all | bytes 4194304 | tf_op jit(solution)/shard_map/spread_solution/all_to_all | solution.py:23
  192.3 0.0 collective-permute-start.1
  192.3 0.0 copy-done
  192.3 0.1 dynamic-slice_bitcast_fusion
  192.4 0.1 broadcast_compare_fusion
  192.5 1.2 select_reduce_fusion
  193.6 0.0 reduce-scatter.2.cloned.1.call-update
  193.7 0.8 copy.36
  194.4 2.2 collective-permute-done.1.other_ref
  196.6 0.0 copy-done.3
  196.6 0.0 copy-done.8
  196.6 0.0 copy-start.1
  196.6 2.5 %copy-done.1 = bf16[32,5,128,128]{3,2,1,0:T(8,128)(2,1)S(1)} copy-done((bf16[32,5,128,128]{3,2,1,0:T(8,128)(2,1)S(1)}, bf16[32,5,128,128]{3,2,1,0:T(8,128)(2,1)}, u32[]{:S(2)}) %copy-start.1) | copy-done | bytes 5242904
  199.1 1.6 copy-done.6
  200.7 12.2 %leaf_backward.1 = bf16[32,128,256]{2,1,0:T(8,128)(2,1)} custom-call(s32[160]{0:T(256)S(1)} %reshape.82.rows_ref, s32[32]{0:T(128)S(1)} %copy-done.8, s32[1]{0:T(128)} %bitcast.parity_ref, bf16[32,128,128]{2,1,0:T(8,128)(2,1)S(1)} %copy-done.3, bf16[32,128,256]{2,1,0:T(8,128)(2,1)S(1)} %copy-done.6, bf16[32,5,128,128]{3,2,1,0:T(8,128)(2,1)S(1)} %copy-done.1, ...), custom_call_target="tpu_custom_call" | custom-call | tf_op jit(solution)/shard_map/leaf_backward/pallas_call | solution.py:136
  212.9 12.7 %reduce-scatter.2.cloned.1.call-done = bf16[1,128,256]{2,1,0:T(8,128)(2,1)} async-done(((bf16[8,128,256]{2,1,0:T(8,128)(2,1)}), bf16[1,128,256]{2,1,0:T(8,128)(2,1)}) %reduce-scatter.2.cloned.1.call-update) | async-done | bytes 65552 | tf_op jit(solution)/shard_map/order_rows/reduce_scatter | solution.py:186
  (5 shorter events, 0.1 us)
Async XLA Ops:
  7.2 185.1 %copy-start = (s32[1,32]{1,0:T(1,128)S(1)}, s32[1,32]{1,0:T(1,128)}, u32[]{:S(2)}) copy-start(s32[1,32]{1,0:T(1,128)} %param.14) | copy-start | bytes 388
  8.1 1.2 copy-start.2
  9.3 1.6 copy-start.4
  10.9 0.7 copy-start.7
  23.5 1.3 copy-start.5
  24.8 4.2 %collective-permute-start = (bf16[32,128,256]{2,1,0:T(8,128)(2,1)S(1)}, bf16[32,128,256]{2,1,0:T(8,128)(2,1)S(1)}, u32[]{:S(2)}, u32[]{:S(2)}) collective-permute-start(bf16[32,128,256]{2,1,0:T(8,128)(2,1)S(1)} %slice.7), channel_id=1, source_target_pairs={{0,32},{32,0},{64,96},{96,64},{128,160},{160,128},{192,224},{224,1... | collective-permute-start | bytes 6291464 | tf_op jit(solution)/shard_map/sum_terms/ppermute | solution.py:28
  60.5 9.7 %copy-start.9 = (bf16[1,128,4096]{2,1,0:T(8,128)(2,1)S(1)}, bf16[1,128,4096]{2,1,0:T(8,128)(2,1)}, u32[]{:S(2)}) copy-start(bf16[1,128,4096]{2,1,0:T(8,128)(2,1)} %param.15) | copy-start | bytes 3145732
  61.7 24.8 %all-to-all-start.1 = ((bf16[8,128,256]{2,1,0:T(8,128)(2,1)}), bf16[8,128,256]{2,1,0:T(8,128)(2,1)S(1)}, u32[]{:S(2)}, u32[]{:S(2)}) async-start(bf16[8,128,256]{2,1,0:T(8,128)(2,1)} %reduce_sum.58), calls=%async_computation.1 | async-start | bytes 1048576 | tf_op jit(solution)/shard_map/sum_terms/all_to_all | solution.py:23
  70.9 19.3 %copy-start.10 = (bf16[1,128,256]{2,1,0:T(8,128)(2,1)S(1)}, bf16[1,128,256]{2,1,0:T(8,128)(2,1)}, u32[]{:S(2)}) copy-start(bf16[1,128,256]{2,1,0:T(8,128)(2,1)} %param.13) | copy-start | bytes 196612
  86.6 16.8 %all-to-all-start.3 = ((bf16[4,128,1024]{1,2,0:T(8,128)(2,1)}), bf16[4,128,1024]{1,2,0:T(8,128)(2,1)S(1)}, u32[]{:S(2)}, u32[]{:S(2)}) async-start(bf16[4,128,1024]{1,2,0:T(8,128)(2,1)} %bitcast.7), calls=%async_computation.3 | async-start | bytes 2097152 | tf_op jit(solution)/shard_map/spread_panels/all_to_all | solution.py:23
  104.1 18.2 %all-to-all-start.2 = ((bf16[8,128,256]{2,1,0:T(8,128)(2,1)}), bf16[8,128,256]{2,1,0:T(8,128)(2,1)S(1)}, u32[]{:S(2)}, u32[]{:S(2)}) async-start(bf16[8,128,256]{2,1,0:T(8,128)(2,1)} %broadcast_in_dim.33), calls=%async_computation.2 | async-start | bytes 1048576 | tf_op jit(solution)/shard_map/separators/all_to_all | solution.py:23
  107.6 118.0 %reduce-scatter.2.cloned.1.call-start = ((), (), s32[]{:S(2)}) async-start(), calls=%async_computation.9 | async-start | bytes 589824 | tf_op jit(solution)/shard_map/order_rows/reduce_scatter | solution.py:186
  169.7 26.9 %copy-start.3 = (bf16[32,128,128]{2,1,0:T(8,128)(2,1)S(1)}, bf16[32,128,128]{2,1,0:T(8,128)(2,1)}, u32[]{:S(2)}) copy-start(bf16[32,128,128]{2,1,0:T(8,128)(2,1)} %inv_ref.3) | copy-start | bytes 3145732
  169.7 26.9 %copy-start.8 = (s32[32]{0:T(128)S(1)}, s32[32]{0:T(128)}, u32[]{:S(2)}) copy-start(s32[32]{0:T(128)} %fill_ref.3) | copy-start | bytes 388
  192.3 4.3 %collective-permute-start.1 = (bf16[32,128,256]{2,1,0:T(8,128)(2,1)S(1)}, bf16[32,128,256]{2,1,0:T(8,128)(2,1)}, u32[]{:S(2)}, u32[]{:S(2)}) collective-permute-start(bf16[32,128,256]{2,1,0:T(8,128)(2,1)S(1)} %all_to_all.45.own_ref), channel_id=1, source_target_pairs={{0,32},{32,0},{64,96},{96,64},{128,160},{160,128},{192,224},{224,1... | collective-permute-start | bytes 6291464 | tf_op jit(solution)/shard_map/spread_solution/ppermute | solution.py:28
  196.6 2.5 %copy-start.1 = (bf16[32,5,128,128]{3,2,1,0:T(8,128)(2,1)S(1)}, bf16[32,5,128,128]{3,2,1,0:T(8,128)(2,1)}, u32[]{:S(2)}) copy-start(bf16[32,5,128,128]{3,2,1,0:T(8,128)(2,1)} %off_ref.3) | copy-start | bytes 15728644
  199.1 1.6 copy-start.6
Sparse Core Ops, SparseCore 0:
  193.8 31.7 reduce-scatter.1

commit v2 on v1

v2 whole, which is shorter than its diff:
```python
import functools

import jax
import jax.numpy as jnp
from jax import lax
from jax.experimental import pallas as pl
from jax.experimental.pallas import tpu as pltpu
from jax.sharding import PartitionSpec as P

X = 4
F32 = jnp.float32
BF16 = jnp.bfloat16


def groups(fronts):
    rows = fronts // X
    along_x = [[z * X + x for x in range(X)] for z in range(rows)]
    along_z = [[z * X + x for z in range(rows)] for x in range(X)]
    return along_x, along_z


def exchange(value, where):
    return lax.all_to_all(value, "front", 0, 0, tiled=True, axis_index_groups=where)


def sibling(value):
    size = lax.axis_size("leaf")
    return lax.ppermute(value, "leaf", [(i, i ^ 1) for i in range(size)])


def place(row, here, seps):
    parity, my_x = here
    rows = seps // X
    local = lax.rem(row, seps)
    away = lax.rem(lax.rem(local, X) + X - my_x, X)
    own = away * rows + local // X
    return jnp.where(row // seps == parity, own, own + seps)


def position():
    return lax.rem(lax.axis_index("leaf"), 2), lax.rem(lax.axis_index("front"), X)


def forward_kernel(per, seps, rows_ref, fill_ref, inv_hbm, rhs_hbm, off_hbm,
                   fwd_hbm, far_own, near_own, far_sib, near_sib,
                   fwd_ref, inv_ref, off_ref, rhs_ref, acc, sems, out_sems):
    leaves, slots, b, _ = off_ref.shape
    rows = seps // X
    here = position()
    copies = []
    for chunk in range(leaves // per):
        some = pl.ds(chunk * per, per)
        copies.append([
            pltpu.make_async_copy(source.at[some], target.at[some], sems.at[chunk, i])
            for i, (source, target) in enumerate(
                ((inv_hbm, inv_ref), (rhs_hbm, rhs_ref), (off_hbm, off_ref)))
        ])
        for copy in copies[-1]:
            copy.start()
    acc[...] = jnp.zeros_like(acc)
    sent = []
    for chunk in range(leaves // per):
        for copy in copies[chunk]:
            copy.wait()
        some = range(chunk * per, chunk * per + per)
        solved = []
        for k in some:
            fwd = jnp.dot(inv_ref[k], rhs_ref[k], preferred_element_type=F32).astype(BF16)
            fwd_ref[k] = fwd
            solved.append(fwd)
        for k, fwd in zip(some, solved):
            products = jnp.dot(off_ref[k].reshape(slots * b, b), fwd, preferred_element_type=F32)
            for p in range(slots):
                spot = jnp.where(p < fill_ref[k], place(rows_ref[p, k], here, seps), 2 * seps)
                acc[spot] += products[p * b:(p + 1) * b]
        some = pl.ds(chunk * per, per)
        sent.append(pltpu.make_async_copy(fwd_ref.at[some], fwd_hbm.at[some], out_sems.at[chunk]))
        sent[-1].start()
    for base, far, near in ((seps, far_sib, near_sib), (0, far_own, near_own)):
        for away, target, spot in ((2, far, 0), (1, near, 0), (3, near, rows), (0, near, 2 * rows)):
            for i in range(rows):
                target[spot + i] = acc[base + away * rows + i].astype(BF16)
    for copy in sent:
        copy.wait()


def forward_leaves(block_rows, fill_count, leaf_inverse, leaf_rhs, off_blocks, seps, per=8):
    leaves, b, r = leaf_rhs.shape
    rows = seps // X
    scalars = pl.BlockSpec(memory_space=pltpu.SMEM)
    anywhere = pl.BlockSpec(memory_space=pl.ANY)
    near_by = pl.BlockSpec(memory_space=pltpu.VMEM)
    far = pltpu.VMEM((rows, b, r), BF16)
    near = pltpu.VMEM((seps - rows, b, r), BF16)
    return pl.pallas_call(
        functools.partial(forward_kernel, per, seps),
        in_specs=[scalars, scalars, anywhere, anywhere, anywhere],
        out_specs=[anywhere] + [near_by] * 4,
        out_shape=[jax.ShapeDtypeStruct((leaves, b, r), BF16), far, near, far, near],
        scratch_shapes=[
            pltpu.VMEM((leaves, b, r), BF16),
            pltpu.VMEM(leaf_inverse.shape, BF16),
            pltpu.VMEM(off_blocks.shape, BF16),
            pltpu.VMEM((leaves, b, r), BF16),
            pltpu.VMEM((2 * seps + 1, b, r), F32),
            pltpu.SemaphoreType.DMA((leaves // per, 3)),
            pltpu.SemaphoreType.DMA((leaves // per,)),
        ],
        compiler_params=pltpu.CompilerParams(vmem_limit_bytes=56 << 20),
    )(block_rows.T, fill_count, leaf_inverse, leaf_rhs, off_blocks)


def hold_kernel(per, *refs):
    count = len(refs) // 2
    sems = refs[-1]
    copies = []
    for i, (source, target) in enumerate(zip(refs[:count], refs[count:])):
        for chunk in range(source.shape[0] // per):
            some = pl.ds(chunk * per, per)
            copies.append(pltpu.make_async_copy(source.at[some], target.at[some], sems.at[i, chunk]))
            copies[-1].start()
    for copy in copies:
        copy.wait()


def hold(*values, per=8):
    anywhere = pl.BlockSpec(memory_space=pl.ANY)
    near_by = pl.BlockSpec(memory_space=pltpu.VMEM)
    return pl.pallas_call(
        functools.partial(hold_kernel, per),
        in_specs=[anywhere] * len(values),
        out_specs=[near_by] * len(values),
        out_shape=[pltpu.VMEM(value.shape, value.dtype) for value in values],
        scratch_shapes=[pltpu.SemaphoreType.DMA((len(values), values[0].shape[0] // per))],
        compiler_params=pltpu.CompilerParams(vmem_limit_bytes=48 << 20),
    )(*values)


def backward_kernel(per, seps, starts, *refs):
    rows_ref, fill_ref, fwd_ref, inv_ref, off_ref = refs[:5]
    pieces = refs[5:5 + len(starts)]
    out_hbm, field, out, sems, out_sems = refs[5 + len(starts):]
    leaves, slots, b, _ = off_ref.shape
    here = position()
    copies = [
        pltpu.make_async_copy(piece, field.at[pl.ds(start, piece.shape[0])], sems.at[i])
        for i, (start, piece) in enumerate(zip(starts, pieces))
    ]
    for copy in copies:
        copy.start()
    field[2 * seps] = jnp.zeros(field.shape[1:], field.dtype)
    for copy in copies:
        copy.wait()
    copies = []
    transposed = (((0,), (0,)), ((), ()))
    for chunk in range(leaves // per):
        some = range(chunk * per, chunk * per + per)
        totals = []
        for k in some:
            picked = jnp.concatenate([
                field[jnp.where(p < fill_ref[k], place(rows_ref[p, k], here, seps), 2 * seps)]
                for p in range(slots)
            ], axis=0)
            pulled = lax.dot_general(off_ref[k].reshape(slots * b, b), picked, transposed,
                                     preferred_element_type=F32)
            totals.append((fwd_ref[k].astype(F32) - pulled).astype(BF16))
        for k, total in zip(some, totals):
            out[k] = lax.dot_general(inv_ref[k], total, transposed, preferred_element_type=F32).astype(BF16)
        some = pl.ds(chunk * per, per)
        copies.append(pltpu.make_async_copy(out.at[some], out_hbm.at[some], out_sems.at[chunk]))
        copies[-1].start()
    for copy in copies:
        copy.wait()


def backward_leaves(block_rows, fill_count, forward, leaf_inverse, off_blocks, starts, pieces, seps, per=8):
    leaves, b, r = forward.shape
    scalars = pl.BlockSpec(memory_space=pltpu.SMEM)
    anywhere = pl.BlockSpec(memory_space=pl.ANY)
    near_by = pl.BlockSpec(memory_space=pltpu.VMEM)
    return pl.pallas_call(
        functools.partial(backward_kernel, per, seps, starts),
        in_specs=[scalars, scalars] + [near_by] * 3 + [anywhere] * len(pieces),
        out_specs=anywhere,
        out_shape=jax.ShapeDtypeStruct((leaves, b, r), BF16),
        scratch_shapes=[
            pltpu.VMEM((2 * seps + 1, b, r), BF16),
            pltpu.VMEM((leaves, b, r), BF16),
            pltpu.SemaphoreType.DMA((len(pieces),)),
            pltpu.SemaphoreType.DMA((leaves // per,)),
        ],
        compiler_params=pltpu.CompilerParams(vmem_limit_bytes=28 << 20),
    )(block_rows.T, fill_count, forward, leaf_inverse, off_blocks, *pieces)


def shifted(value, by, fronts):
    return lax.ppermute(value, "front", [(i, i // X * X + (i + by) % X) for i in range(fronts)])


def added(*values):
    return sum(v.astype(F32) for v in values)


def local(kernel, outs, *values):
    near_by = pl.BlockSpec(memory_space=pltpu.VMEM)
    return pl.pallas_call(
        kernel,
        in_specs=[near_by] * len(values),
        out_specs=[near_by] * len(outs),
        out_shape=[jax.ShapeDtypeStruct(shape, BF16) for shape in outs],
    )(*values)


def split_kernel(panel_ref, *out_refs):
    b = panel_ref.shape[1]
    my_x = lax.rem(lax.axis_index("front"), X)
    for k, out in enumerate(out_refs):
        column = lax.rem(my_x + k, X)
        for z in range(out.shape[1] // b):
            start = pl.multiple_of((z * X + column) * b, b)
            out[:, z * b:(z + 1) * b] = panel_ref[0, :, pl.ds(start, b)]


def join_kernel(p0, p1, p2, p3, out_ref):
    b = p0.shape[0]
    my_x = lax.rem(lax.axis_index("front"), X)
    for k, panel in enumerate((p0, p1, p2, p3)):
        start = pl.multiple_of(lax.rem(my_x + X - k, X) * b, b)
        out_ref[pl.ds(start, b), :] = panel[...]


def on_device(
    leaf_inverse, leaf_rhs, off_blocks, block_rows, fill_count, sep_rhs, panel_order, sep_inverse
):
    b = leaf_inverse.shape[1]
    r = leaf_rhs.shape[2]
    seps = lax.axis_size("front")
    rows = seps // X
    half = rows // 2
    along_x, along_z = groups(seps)
    me = lax.axis_index("front")
    my_x, my_z = me % X, me // X
    shift = functools.partial(shifted, fronts=seps)
    together = lax.optimization_barrier

    with jax.named_scope("leaf_forward"):
        forward, far, near, far_sib, near_sib = forward_leaves(
            block_rows, fill_count, leaf_inverse, leaf_rhs, off_blocks, seps
        )
    with jax.named_scope("sum_terms"):
        far_in = sibling(far_sib)
        far_in, near_sib = together((far_in, near_sib))
        near_in = sibling(near_sib)
        right2 = shift(added(far[:half], far_in[:half]).astype(BF16), 1)
        left2 = shift(added(far[half:], far_in[half:]).astype(BF16), -1)

        def own(at):
            return added(near[at:at + rows], near_in[at:at + rows])

        none = ((0, 0), (0, 0))
        right2 = jnp.pad(right2.astype(F32), ((0, half), *none))
        left2 = jnp.pad(left2.astype(F32), ((half, 0), *none))
        from_left = shift((own(0) + right2).astype(BF16), 1)
        from_right = shift((own(rows) + left2).astype(BF16), -1)
        column = (own(2 * rows) + added(from_left, from_right)).astype(BF16)
    with jax.named_scope("spread_panels"):
        far_in, sep_inverse = together((far_in, sep_inverse))
        panels = list(local(split_kernel, [(b, rows * b)] * X, sep_inverse))
        panels[1], panels[3], column = together((panels[1], panels[3], column))
        panels[1], panels[3] = shift(panels[1], 1), shift(panels[3], -1)
    with jax.named_scope("sum_terms"):
        column = exchange(column, along_z)
        column, *panels = together((column, *panels))
        summed = added(*column)
    with jax.named_scope("spread_panels"):
        panels[2] = shift(panels[2], 2)
        (panel,) = local(join_kernel, [(X * b, rows * b)], *panels)
    with jax.named_scope("separators"):
        separator_in = (sep_rhs[0].astype(F32) - summed).astype(BF16)
        right = exchange(jnp.broadcast_to(separator_in[None], (rows, b, r)), along_z)
        part = jnp.dot(panel, right.reshape(rows * b, r), preferred_element_type=F32).astype(BF16)
        parts = exchange(jnp.broadcast_to(part[None], (X, X * b, r)).reshape(X * X * b, r), along_x)
        solved_rows = added(*parts.reshape(X, X * b, r)).astype(BF16)
        adjoint = lax.dot_general(panel, solved_rows, (((0,), (0,)), ((), ())), preferred_element_type=F32)
        sep_solution = added(*exchange(adjoint.reshape(rows, b, r).astype(BF16), along_z))
    with jax.named_scope("order_rows"):
        held = lax.dynamic_slice_in_dim(panel_order[0], my_z * X, X)
        wanted = jnp.arange(rows, dtype=jnp.int32) * X + my_x
        chosen = held[None, :] == wanted[:, None]
        blocks = jnp.where(
            chosen[:, :, None, None], solved_rows.reshape(1, X, b, r), jnp.zeros((), BF16)
        ).astype(F32).sum(1).astype(BF16)
    with jax.named_scope("spread_solution"):
        solved = sep_solution.astype(BF16)
        column = exchange(jnp.broadcast_to(solved[None], (rows, b, r)), along_z)
        slot = jnp.argmax(panel_order[0] == me).astype(jnp.int32)
        column, blocks, slot = together((column, blocks, slot))
        behind, ahead = shift(column, 1), shift(column, -1)
        far_low, far_high = shift(behind[:half], 1), shift(ahead[half:], -1)
    with jax.named_scope("order_rows"):
        blocks = exchange(blocks, along_z)
        far_low, far_high, blocks = together((far_low, far_high, blocks))
        sep_forward = lax.dynamic_slice_in_dim(blocks, slot // X, 1)
    with jax.named_scope("leaf_backward"):
        field = jnp.concatenate([column, ahead, far_low, far_high, behind])
        field, *leaves = together((field, forward, leaf_inverse, off_blocks))
        other = sibling(field)
        leaf_solution = backward_leaves(
            block_rows, fill_count, *hold(*leaves), [0, seps], [field, other], seps
        )
    return leaf_solution, sep_forward, sep_solution[None]


def solution(mesh):
    both = ("leaf", "front")
    return jax.shard_map(
        on_device,
        mesh=mesh,
        in_specs=(
            P(both, None, None),
            P(both, None, None),
            P(both, None, None, None),
            P(both, None),
            P(both),
            P(both, None, None),
            P("leaf", None),
            P(both, None, None),
        ),
        out_specs=(P(both, None, None), P(both, None, None), P(both, None, None)),
        check_vma=False,
    )
```

time: 233 us -> 181 us (0.78)
  blocking collectives: 98.7 us -> 16.4 us
  starting transfers between devices: 15.5 us -> 42.1 us
  waiting for transfers between devices: 60.9 us -> 77.8 us
  between operations: 14.3 us -> 3.83 us
  local copies, waits for them, and re-layouts: 14.3 us -> 6.7 us
  other arithmetic: 3.73 us -> 6.71 us
    all_to_all x5 -> x1, blocking collectives: 98.7 us -> 16.4 us  [exchange(): lax.all_to_all(value, 'front', 0, 0, tiled=True, axis_index_groups=where)]
    ppermute x0 -> x11, waiting for transfers between devices: none -> 40.5 us  [shifted(): lax.ppermute(value, 'front', [(i, i // X * X + (i + by) % X) for i in ran...]
    ppermute x0 -> x11, starting transfers between devices: none -> 18.6 us  [shifted(): lax.ppermute(value, 'front', [(i, i // X * X + (i + by) % X) for i in ran...]
    reduce_scatter x1 -> x0, waiting for transfers between devices: 12.7 us -> none  [on_device(): lax.psum_scatter(blocks, 'front', scatter_dimension=0, tiled=True, axis_i...]
    unnamed x25 -> x24, local copies, waits for them, and re-layouts: 10.9 us -> 1.8 us
    all_to_all x3 -> x5, starting transfers between devices: 15.5 us -> 23.2 us  [exchange(): lax.all_to_all(value, 'front', 0, 0, tiled=True, axis_index_groups=where)]
    all_to_all x3 -> x5, waiting for transfers between devices: 41.8 us -> 35.4 us  [exchange(): lax.all_to_all(value, 'front', 0, 0, tiled=True, axis_index_groups=where)]
    ppermute x2 -> x3, waiting for transfers between devices: 6.32 us -> 1.9 us  [sibling(): return lax.ppermute(value, 'leaf', [(i, i ^ 1) for i in range(size)])]
  transfers between devices with their start and end apart: 6 -> 19, of which waited for: 6 -> 11; matrix products, arithmetic and copies ran while one was open for 2% -> 2% of each run, Pallas kernels for 5% -> 5%
where the time goes in v2:
time: 181 us; the launch traced here: 179 us
  waiting for transfers between devices  77.8 us (43%)
  starting transfers between devices  42.1 us (23%)
  Pallas kernels  23.2 us (13%)
  blocking collectives  16.4 us (9%)
  other arithmetic  6.71 us (4%)
  local copies, waits for them, and re-layouts  6.7 us (4%)
  between operations  3.83 us (2%)
  matrix products  2.09 us (1%)
    ppermute x11, waiting for transfers between devices, shifted(): lax.ppermute(value, 'front', [(i, i // X * X + (i + by) % X) for i in ran...  40.5 us
    all_to_all x5, waiting for transfers between devices, exchange(): lax.all_to_all(value, 'front', 0, 0, tiled=True, axis_index_groups=where)  35.4 us
    all_to_all x5, starting transfers between devices, exchange(): lax.all_to_all(value, 'front', 0, 0, tiled=True, axis_index_groups=where)  23.2 us
    ppermute x11, starting transfers between devices, shifted(): lax.ppermute(value, 'front', [(i, i // X * X + (i + by) % X) for i in ran...  18.6 us
    all_to_all x1, blocking collectives, exchange(): lax.all_to_all(value, 'front', 0, 0, tiled=True, axis_index_groups=where)  16.4 us
    pallas_call x1, Pallas kernels, forward_leaves(): pl.pallas_call(functools.partial(forward_kernel, per, seps), in_specs=[sc...  8.47 us
    pallas_call x1, Pallas kernels, backward_leaves(): pl.pallas_call(functools.partial(backward_kernel, per, seps, starts), in_...  6.47 us
    pallas_call x2, Pallas kernels, local(): pl.pallas_call(kernel, in_specs=[near_by] * len(values), out_specs=[near_...  4.77 us
  transfers between devices with their start and end apart: 19, of which 11 were waited for; matrix products, arithmetic and copies ran while one was open for 2% of the time, Pallas kernels for 5%

profile of v2, /device:TPU:8, one launch (start us, length us, event | category | flops | bytes accessed | tf_op | source)
XLA Modules:
  0.0 178.9 jit_solution(894853216545659644)
XLA Ops:
  0.6 8.5 %leaf_forward.1 = (bf16[32,128,256]{2,1,0:T(8,128)(2,1)}, bf16[8,128,256]{2,1,0:T(8,128)(2,1)S(1)}, bf16[24,128,256]{2,1,0:T(8,128)(2,1)S(1)}, bf16[8,128,256]{2,1,0:T(8,128)(2,1)S(1)}, bf16[24,128,256]{2,1,0:T(8,128)(2,1)S(1)}) custom-call(s32[5,32]{1,0:T(8,128)} %bitcast.20, s32[32]{0:T(128)} %refs_1_.2, bf16[32,128,128]{2,1,0:T(8,128)(2,1)} %refs_1_.1, ...), custom_call_target="tpu_custom_call" | custom-call | tf_op jit(solution)/shard_map/leaf_forward/pallas_call | solution.py:95
  9.1 0.1 collective-permute-start
  9.2 1.9 %collective-permute-done = bf16[8,128,256]{2,1,0:T(8,128)(2,1)S(1)} collective-permute-done((bf16[8,128,256]{2,1,0:T(8,128)(2,1)S(1)}, bf16[8,128,256]{2,1,0:T(8,128)(2,1)S(1)}, u32[]{:S(2)}, u32[]{:S(2)}) %collective-permute-start) | collective-permute-done | bytes 524320 | tf_op jit(solution)/shard_map/sum_terms/ppermute | solution.py:28
  11.1 0.1 collective-permute-start.1
  11.2 0.1 add_convert_fusion.5
  11.4 1.6 collective-permute-start.2
  13.0 1.7 collective-permute-start.4
  14.7 6.5 %collective-permute-done.2 = bf16[4,128,256]{2,1,0:T(8,128)(2,1)S(1)} collective-permute-done((bf16[4,128,256]{2,1,0:T(8,128)(2,1)S(1)}, bf16[4,128,256]{2,1,0:T(8,128)(2,1)S(1)}, u32[]{:S(2)}, u32[]{:S(2)}) %collective-permute-start.2) | collective-permute-done | bytes 262176 | tf_op jit(solution)/shard_map/sum_terms/ppermute | solution.py:197
  21.2 0.0 collective-permute-done.4
  21.3 0.0 collective-permute-done.1
  21.3 1.4 add_convert_fusion.2
  22.6 1.5 collective-permute-start.3
  24.1 1.8 collective-permute-start.5
  25.9 2.5 %spread_panels.2 = (bf16[128,1024]{1,0:T(8,128)(2,1)}, bf16[128,1024]{1,0:T(8,128)(2,1)}, bf16[128,1024]{1,0:T(8,128)(2,1)}, bf16[128,1024]{1,0:T(8,128)(2,1)}) custom-call(bf16[1,128,4096]{2,1,0:T(8,128)(2,1)} %panel_ref), custom_call_target="tpu_custom_call" | custom-call | tf_op jit(solution)/shard_map/spread_panels/pallas_call | solution.py:206
  28.3 9.2 %collective-permute-done.3 = bf16[8,128,256]{2,1,0:T(8,128)(2,1)} collective-permute-done((bf16[8,128,256]{2,1,0:T(8,128)(2,1)}, bf16[8,128,256]{2,1,0:T(8,128)(2,1)}, u32[]{:S(2)}, u32[]{:S(2)}) %collective-permute-start.3) | collective-permute-done | bytes 524320 | tf_op jit(solution)/shard_map/sum_terms/ppermute | solution.py:197
  37.5 0.0 collective-permute-done.5
  37.5 2.3 %add_convert_fusion = bf16[8,128,256]{2,1,0:T(8,128)(2,1)} fusion(bf16[8,128,256]{2,1,0:T(8,128)(2,1)} %collective-permute-done.5, bf16[8,128,256]{2,1,0:T(8,128)(2,1)} %collective-permute-done.3, bf16[24,128,256]{2,1,0:T(8,128)(2,1)S(1)} %collective-permute-done.1, bf16[24,128,256]{2,1,0:T(8,128)(2,1)S(1)} %get-tuple-element.43), kind=kLoop, calls=%fused_computation.3 | loop fusion | flops 2097152 | bytes 2621440 | tf_op jit(solution)/shard_map/sum_terms/convert_element_type | solution.py:265
  39.8 8.6 %all-to-all-start = ((bf16[8,128,256]{2,1,0:T(8,128)(2,1)}), bf16[8,128,256]{2,1,0:T(8,128)(2,1)S(1)}, u32[]{:S(2)}, u32[]{:S(2)}) async-start(bf16[8,128,256]{2,1,0:T(8,128)(2,1)} %add_convert_fusion), calls=%async_computation | async-start | bytes 1048576 | tf_op jit(solution)/shard_map/sum_terms/all_to_all | solution.py:23
  48.4 0.9 collective-permute-start.6
  49.3 2.3 %collective-permute-start.7 = (bf16[128,1024]{1,0:T(8,128)(2,1)S(1)}, bf16[128,1024]{1,0:T(8,128)(2,1)S(1)}, u32[]{:S(2)}, u32[]{:S(2)}) collective-permute-start(bf16[128,1024]{1,0:T(8,128)(2,1)S(1)} %copy-done.9), channel_id=1, source_target_pairs={{0,3},{1,0},{2,1},{3,2},{4,7},{5,4},{6,5},{7,6},{8,11},{9,8},{10,9... | collective-permute-start | bytes 786440 | tf_op jit(solution)/shard_map/spread_panels/ppermute | solution.py:197
  51.7 4.7 %collective-permute-done.6.p1 = bf16[128,1024]{1,0:T(8,128)(2,1)S(1)} collective-permute-done((bf16[128,1024]{1,0:T(8,128)(2,1)}, bf16[128,1024]{1,0:T(8,128)(2,1)S(1)}, u32[]{:S(2)}, u32[]{:S(2)}) %collective-permute-start.6) | collective-permute-done | bytes 262176 | tf_op jit(solution)/shard_map/spread_panels/ppermute | solution.py:197
  56.4 8.3 %all-to-all-done = bf16[8,128,256]{2,1,0:T(8,128)(2,1)S(1)} async-done(((bf16[8,128,256]{2,1,0:T(8,128)(2,1)}), bf16[8,128,256]{2,1,0:T(8,128)(2,1)S(1)}, u32[]{:S(2)}, u32[]{:S(2)}) %all-to-all-start) | async-done | bytes 524320 | tf_op jit(solution)/shard_map/sum_terms/all_to_all | solution.py:23
  64.7 0.1 fusion.1
  64.8 0.9 broadcast_in_dim.47
  65.6 3.5 %all-to-all-start.1 = ((bf16[8,128,256]{2,1,0:T(8,128)(2,1)}), bf16[8,128,256]{2,1,0:T(8,128)(2,1)S(1)}, u32[]{:S(2)}, u32[]{:S(2)}) async-start(bf16[8,128,256]{2,1,0:T(8,128)(2,1)} %broadcast_in_dim.47), calls=%async_computation.1 | async-start | bytes 1048576 | tf_op jit(solution)/shard_map/separators/all_to_all | solution.py:23
  69.2 2.1 %collective-permute-start.8 = (bf16[128,1024]{1,0:T(8,128)(2,1)S(1)}, bf16[128,1024]{1,0:T(8,128)(2,1)S(1)}, u32[]{:S(2)}, u32[]{:S(2)}) collective-permute-start(bf16[128,1024]{1,0:T(8,128)(2,1)S(1)} %copy-done.8), channel_id=1, source_target_pairs={{0,2},{1,3},{2,0},{3,1},{4,6},{5,7},{6,4},{7,5},{8,10},{9,11},{10,... | collective-permute-start | bytes 786440 | tf_op jit(solution)/shard_map/spread_panels/ppermute | solution.py:197
  71.2 5.9 %collective-permute-done.8.p2 = bf16[128,1024]{1,0:T(8,128)(2,1)S(1)} collective-permute-done((bf16[128,1024]{1,0:T(8,128)(2,1)S(1)}, bf16[128,1024]{1,0:T(8,128)(2,1)S(1)}, u32[]{:S(2)}, u32[]{:S(2)}) %collective-permute-start.8) | collective-permute-done | bytes 262176 | tf_op jit(solution)/shard_map/spread_panels/ppermute | solution.py:197
  77.1 0.7 copy-done.5
  77.8 2.3 %spread_panels.3 = bf16[512,1024]{1,0:T(8,128)(2,1)} custom-call(bf16[128,1024]{1,0:T(8,128)(2,1)} %get-tuple-element.51.p0, bf16[128,1024]{1,0:T(8,128)(2,1)} %copy-done.3, bf16[128,1024]{1,0:T(8,128)(2,1)} %copy-done.5, bf16[128,1024]{1,0:T(8,128)(2,1)} %copy-done.4), custom_call_target="tpu_custom_call" | custom-call | tf_op jit(solution)/shard_map/spread_panels/pallas_call | solution.py:206
  80.1 4.5 %all-to-all-done.1 = bf16[8,128,256]{2,1,0:T(8,128)(2,1)S(1)} async-done(((bf16[8,128,256]{2,1,0:T(8,128)(2,1)}), bf16[8,128,256]{2,1,0:T(8,128)(2,1)S(1)}, u32[]{:S(2)}, u32[]{:S(2)}) %all-to-all-start.1) | async-done | bytes 524320 | tf_op jit(solution)/shard_map/separators/all_to_all | solution.py:23
  84.6 1.7 convolution_convert_fusion.1
  86.3 1.0 broadcast_in_dim.48
  87.3 3.5 %all-to-all-start.2 = ((bf16[4,512,256]{2,1,0:T(8,128)(2,1)}), bf16[4,512,256]{2,1,0:T(8,128)(2,1)S(1)}, u32[]{:S(2)}, u32[]{:S(2)}) async-start(bf16[4,512,256]{2,1,0:T(8,128)(2,1)} %broadcast_in_dim.48), calls=%async_computation.2 | async-start | bytes 2097152 | tf_op jit(solution)/shard_map/separators/all_to_all | solution.py:23
  90.8 0.5 copy.13
  91.4 11.5 %all-to-all-done.2 = bf16[4,512,256]{2,1,0:T(8,128)(2,1)S(1)} async-done(((bf16[4,512,256]{2,1,0:T(8,128)(2,1)}), bf16[4,512,256]{2,1,0:T(8,128)(2,1)S(1)}, u32[]{:S(2)}, u32[]{:S(2)}) %all-to-all-start.2) | async-done | bytes 1048608 | tf_op jit(solution)/shard_map/separators/all_to_all | solution.py:23
  102.9 0.1 add_convert_fusion.3
  103.0 0.4 convolution_convert_fusion
  103.5 0.0 copy-start.7
  103.5 16.4 %all_to_all.31 = bf16[8,128,256]{2,1,0:T(8,128)(2,1)S(1)} all-to-all(bf16[8,128,256]{2,1,0:T(8,128)(2,1)S(1)} %convolution_convert_fusion), channel_id=1, replica_groups={{0,4,8,12,16,20,24,28},{1,5,9,13,17,21,25,29},{2,6,10,14,18,22,26,30},{..., dimensions={0} | all-to-all | bytes 1048576 | tf_op jit(solution)/shard_map/separators/all_to_all | solution.py:23
  119.9 0.7 convert_bitcast_fusion
  120.6 0.8 broadcast_in_dim.50
  121.4 3.5 %all-to-all-start.4 = ((bf16[8,128,256]{2,1,0:T(8,128)(2,1)}), bf16[8,128,256]{2,1,0:T(8,128)(2,1)S(1)}, u32[]{:S(2)}, u32[]{:S(2)}) async-start(bf16[8,128,256]{2,1,0:T(8,128)(2,1)} %broadcast_in_dim.50), calls=%async_computation.4 | async-start | bytes 1048576 | tf_op jit(solution)/shard_map/spread_solution/all_to_all | solution.py:23
  125.0 0.1 dynamic-slice_bitcast_fusion
  125.1 0.7 bitcast_reduce_fusion
  125.8 0.1 broadcast_compare_fusion
  125.9 1.2 select_reduce_fusion
  127.1 11.1 %all-to-all-done.4 = bf16[8,128,256]{2,1,0:T(8,128)(2,1)S(1)} async-done(((bf16[8,128,256]{2,1,0:T(8,128)(2,1)}), bf16[8,128,256]{2,1,0:T(8,128)(2,1)S(1)}, u32[]{:S(2)}, u32[]{:S(2)}) %all-to-all-start.4) | async-done | bytes 524320 | tf_op jit(solution)/shard_map/spread_solution/all_to_all | solution.py:23
  138.1 4.2 %all-to-all-start.5 = ((bf16[8,128,256]{2,1,0:T(8,128)(2,1)}), bf16[8,128,256]{2,1,0:T(8,128)(2,1)}, u32[]{:S(2)}, u32[]{:S(2)}) async-start(bf16[8,128,256]{2,1,0:T(8,128)(2,1)} %select_reduce_fusion), calls=%async_computation.5 | async-start | bytes 1048576 | tf_op jit(solution)/shard_map/order_rows/all_to_all | solution.py:23
  142.3 0.6 collective-permute-start.10
  143.0 2.7 %collective-permute-start.9 = (bf16[8,128,256]{2,1,0:T(8,128)(2,1)S(1)}, bf16[8,128,256]{2,1,0:T(8,128)(2,1)S(1)}, u32[]{:S(2)}, u32[]{:S(2)}) collective-permute-start(bf16[8,128,256]{2,1,0:T(8,128)(2,1)S(1)} %all-to-all-done.4), channel_id=1, source_target_pairs={{0,3},{1,0},{2,1},{3,2},{4,7},{5,4},{6,5},{7,6},{8,11},{9,8},{10,9... | collective-permute-start | bytes 1572872 | tf_op jit(solution)/shard_map/spread_solution/ppermute | solution.py:197
  145.6 10.0 %collective-permute-done.10 = bf16[8,128,256]{2,1,0:T(8,128)(2,1)S(1)} collective-permute-done((bf16[8,128,256]{2,1,0:T(8,128)(2,1)S(1)}, bf16[8,128,256]{2,1,0:T(8,128)(2,1)S(1)}, u32[]{:S(2)}, u32[]{:S(2)}) %collective-permute-start.10) | collective-permute-done | bytes 524320 | tf_op jit(solution)/shard_map/spread_solution/ppermute | solution.py:197
  155.6 0.1 collective-permute-start.11
  155.7 0.0 collective-permute-done.9
  155.7 3.3 %collective-permute-start.12 = (bf16[4,128,256]{2,1,0:T(8,128)(2,1)S(1)}, bf16[4,128,256]{2,1,0:T(8,128)(2,1)}, u32[]{:S(2)}, u32[]{:S(2)}) collective-permute-start(bf16[4,128,256]{2,1,0:T(8,128)(2,1)S(1)} %slice.60), channel_id=1, source_target_pairs={{0,3},{1,0},{2,1},{3,2},{4,7},{5,4},{6,5},{7,6},{8,11},{9,8},{10,9... | collective-permute-start | bytes 786440 | tf_op jit(solution)/shard_map/spread_solution/ppermute | solution.py:197
  159.1 4.2 %collective-permute-done.11 = bf16[4,128,256]{2,1,0:T(8,128)(2,1)S(1)} collective-permute-done((bf16[4,128,256]{2,1,0:T(8,128)(2,1)S(1)}, bf16[4,128,256]{2,1,0:T(8,128)(2,1)S(1)}, u32[]{:S(2)}, u32[]{:S(2)}) %collective-permute-start.11) | collective-permute-done | bytes 262176 | tf_op jit(solution)/shard_map/spread_solution/ppermute | solution.py:197
  163.3 0.0 collective-permute-done.12
  163.3 1.0 constant_dynamic-update-slice_fusion.1
  164.3 0.1 collective-permute-start.13
  167.2 0.0 copy-start
  167.2 0.0 copy-start.1
  167.2 3.5 %leaf_backward.2 = (bf16[32,128,256]{2,1,0:T(8,128)(2,1)S(1)}, bf16[32,128,128]{2,1,0:T(8,128)(2,1)S(1)}, bf16[32,5,128,128]{3,2,1,0:T(8,128)(2,1)S(1)}) custom-call(bf16[32,128,256]{2,1,0:T(8,128)(2,1)} %get-tuple-element.62.refs_0_, bf16[32,128,128]{2,1,0:T(8,128)(2,1)} %refs_1_.1, bf16[32,5,128,128]{3,2,1,0:T(8,128)(2,1)} %refs_2_), custom_call_target="tpu_custom_call" | custom-call | tf_op jit(solution)/shard_map/leaf_backward/pallas_call | solution.py:129
  170.8 1.5 constant_dynamic-slice_fusion
  172.2 0.0 collective-permute-done.13.refs_6_
  172.3 6.5 %leaf_backward.3 = bf16[32,128,256]{2,1,0:T(8,128)(2,1)} custom-call(s32[5,32]{1,0:T(8,128)S(1)} %bitcast.21, s32[32]{0:T(128)S(1)} %copy-done.1, bf16[32,128,256]{2,1,0:T(8,128)(2,1)S(1)} %get-tuple-element.65.refs_2_, bf16[32,128,128]{2,1,0:T(8,128)(2,1)S(1)} %get-tuple-element.66.refs_3_, bf16[32,5,128,128]{3,2,1,0:T(8,128)(2,1)S(1)} %get-tuple-element.67.refs_4_, ...), custom_call_target="tpu_custom_call" | custom-call | tf_op jit(solution)/shard_map/leaf_backward/pallas_call | solution.py:181
  (25 shorter events, 0.2 us)
Async XLA Ops:
  9.1 2.0 %collective-permute-start = (bf16[8,128,256]{2,1,0:T(8,128)(2,1)S(1)}, bf16[8,128,256]{2,1,0:T(8,128)(2,1)S(1)}, u32[]{:S(2)}, u32[]{:S(2)}) collective-permute-start(bf16[8,128,256]{2,1,0:T(8,128)(2,1)S(1)} %get-tuple-element.37), channel_id=1, source_target_pairs={{0,32},{32,0},{64,96},{96,64},{128,160},{160,128},{192,224},{224,1... | collective-permute-start | bytes 1572872 | tf_op jit(solution)/shard_map/sum_terms/ppermute | solution.py:28
  11.1 10.2 %collective-permute-start.1 = (bf16[24,128,256]{2,1,0:T(8,128)(2,1)S(1)}, bf16[24,128,256]{2,1,0:T(8,128)(2,1)S(1)}, u32[]{:S(2)}, u32[]{:S(2)}) collective-permute-start(bf16[24,128,256]{2,1,0:T(8,128)(2,1)S(1)} %get-tuple-element.44), channel_id=1, source_target_pairs={{0,32},{32,0},{64,96},{96,64},{128,160},{160,128},{192,224},{224,1... | collective-permute-start | bytes 4718600 | tf_op jit(solution)/shard_map/sum_terms/ppermute | solution.py:28
  11.4 9.9 %collective-permute-start.2 = (bf16[4,128,256]{2,1,0:T(8,128)(2,1)S(1)}, bf16[4,128,256]{2,1,0:T(8,128)(2,1)S(1)}, u32[]{:S(2)}, u32[]{:S(2)}) collective-permute-start(bf16[4,128,256]{2,1,0:T(8,128)(2,1)S(1)} %get-tuple-element.75), channel_id=1, source_target_pairs={{0,1},{1,2},{2,3},{3,0},{4,5},{5,6},{6,7},{7,4},{8,9},{9,10},{10,1... | collective-permute-start | bytes 786440 | tf_op jit(solution)/shard_map/sum_terms/ppermute | solution.py:197
  13.0 8.3 %collective-permute-start.4 = (bf16[4,128,256]{2,1,0:T(8,128)(2,1)S(1)}, bf16[4,128,256]{2,1,0:T(8,128)(2,1)S(1)}, u32[]{:S(2)}, u32[]{:S(2)}) collective-permute-start(bf16[4,128,256]{2,1,0:T(8,128)(2,1)S(1)} %get-tuple-element.76), channel_id=1, source_target_pairs={{0,3},{1,0},{2,1},{3,2},{4,7},{5,4},{6,5},{7,6},{8,11},{9,8},{10,9... | collective-permute-start | bytes 786440 | tf_op jit(solution)/shard_map/sum_terms/ppermute | solution.py:197
  22.6 14.9 %collective-permute-start.3 = (bf16[8,128,256]{2,1,0:T(8,128)(2,1)}, bf16[8,128,256]{2,1,0:T(8,128)(2,1)}, u32[]{:S(2)}, u32[]{:S(2)}) collective-permute-start(bf16[8,128,256]{2,1,0:T(8,128)(2,1)} %get-tuple-element.73), channel_id=1, source_target_pairs={{0,1},{1,2},{2,3},{3,0},{4,5},{5,6},{6,7},{7,4},{8,9},{9,10},{10,1... | collective-permute-start | bytes 1572872 | tf_op jit(solution)/shard_map/sum_terms/ppermute | solution.py:197
  24.1 13.4 %collective-permute-start.5 = (bf16[8,128,256]{2,1,0:T(8,128)(2,1)}, bf16[8,128,256]{2,1,0:T(8,128)(2,1)}, u32[]{:S(2)}, u32[]{:S(2)}) collective-permute-start(bf16[8,128,256]{2,1,0:T(8,128)(2,1)} %get-tuple-element.74), channel_id=1, source_target_pairs={{0,3},{1,0},{2,1},{3,2},{4,7},{5,4},{6,5},{7,6},{8,11},{9,8},{10,9... | collective-permute-start | bytes 1572872 | tf_op jit(solution)/shard_map/sum_terms/ppermute | solution.py:197
  28.3 21.0 %copy-start.9 = (bf16[128,1024]{1,0:T(8,128)(2,1)S(1)}, bf16[128,1024]{1,0:T(8,128)(2,1)}, u32[]{:S(2)}) copy-start(bf16[128,1024]{1,0:T(8,128)(2,1)} %get-tuple-element.50) | copy-start | bytes 786436
  28.3 36.4 %copy-start.6 = (bf16[1,128,256]{2,1,0:T(8,128)(2,1)S(1)}, bf16[1,128,256]{2,1,0:T(8,128)(2,1)}, u32[]{:S(2)}) copy-start(bf16[1,128,256]{2,1,0:T(8,128)(2,1)} %param.13) | copy-start | bytes 196612
  39.8 29.3 %copy-start.8 = (bf16[128,1024]{1,0:T(8,128)(2,1)S(1)}, bf16[128,1024]{1,0:T(8,128)(2,1)}, u32[]{:S(2)}) copy-start(bf16[128,1024]{1,0:T(8,128)(2,1)} %get-tuple-element.53) | copy-start | bytes 786436
  39.8 24.9 %all-to-all-start = ((bf16[8,128,256]{2,1,0:T(8,128)(2,1)}), bf16[8,128,256]{2,1,0:T(8,128)(2,1)S(1)}, u32[]{:S(2)}, u32[]{:S(2)}) async-start(bf16[8,128,256]{2,1,0:T(8,128)(2,1)} %add_convert_fusion), calls=%async_computation | async-start | bytes 1048576 | tf_op jit(solution)/shard_map/sum_terms/all_to_all | solution.py:23
  48.4 8.0 %collective-permute-start.6 = (bf16[128,1024]{1,0:T(8,128)(2,1)}, bf16[128,1024]{1,0:T(8,128)(2,1)S(1)}, u32[]{:S(2)}, u32[]{:S(2)}) collective-permute-start(bf16[128,1024]{1,0:T(8,128)(2,1)} %get-tuple-element.48), channel_id=1, source_target_pairs={{0,1},{1,2},{2,3},{3,0},{4,5},{5,6},{6,7},{7,4},{8,9},{9,10},{10,1... | collective-permute-start | bytes 786440 | tf_op jit(solution)/shard_map/spread_panels/ppermute | solution.py:197
  49.3 7.1 %collective-permute-start.7 = (bf16[128,1024]{1,0:T(8,128)(2,1)S(1)}, bf16[128,1024]{1,0:T(8,128)(2,1)S(1)}, u32[]{:S(2)}, u32[]{:S(2)}) collective-permute-start(bf16[128,1024]{1,0:T(8,128)(2,1)S(1)} %copy-done.9), channel_id=1, source_target_pairs={{0,3},{1,0},{2,1},{3,2},{4,7},{5,4},{6,5},{7,6},{8,11},{9,8},{10,9... | collective-permute-start | bytes 786440 | tf_op jit(solution)/shard_map/spread_panels/ppermute | solution.py:197
  56.4 20.7 %copy-start.3 = (bf16[128,1024]{1,0:T(8,128)(2,1)}, bf16[128,1024]{1,0:T(8,128)(2,1)S(1)}, u32[]{:S(2)}) copy-start(bf16[128,1024]{1,0:T(8,128)(2,1)S(1)} %collective-permute-done.6.p1) | copy-start | bytes 786436
  56.4 20.7 %copy-start.4 = (bf16[128,1024]{1,0:T(8,128)(2,1)}, bf16[128,1024]{1,0:T(8,128)(2,1)S(1)}, u32[]{:S(2)}) copy-start(bf16[128,1024]{1,0:T(8,128)(2,1)S(1)} %collective-permute-done.7.p3) | copy-start | bytes 786436
  65.6 19.0 %all-to-all-start.1 = ((bf16[8,128,256]{2,1,0:T(8,128)(2,1)}), bf16[8,128,256]{2,1,0:T(8,128)(2,1)S(1)}, u32[]{:S(2)}, u32[]{:S(2)}) async-start(bf16[8,128,256]{2,1,0:T(8,128)(2,1)} %broadcast_in_dim.47), calls=%async_computation.1 | async-start | bytes 1048576 | tf_op jit(solution)/shard_map/separators/all_to_all | solution.py:23
  69.2 8.0 %collective-permute-start.8 = (bf16[128,1024]{1,0:T(8,128)(2,1)S(1)}, bf16[128,1024]{1,0:T(8,128)(2,1)S(1)}, u32[]{:S(2)}, u32[]{:S(2)}) collective-permute-start(bf16[128,1024]{1,0:T(8,128)(2,1)S(1)} %copy-done.8), channel_id=1, source_target_pairs={{0,2},{1,3},{2,0},{3,1},{4,6},{5,7},{6,4},{7,5},{8,10},{9,11},{10,... | collective-permute-start | bytes 786440 | tf_op jit(solution)/shard_map/spread_panels/ppermute | solution.py:197
  77.1 0.7 copy-start.5
  86.3 4.6 %copy-start.2 = (bf16[512,1024]{1,0:T(8,128)(2,1)S(1)}, bf16[512,1024]{1,0:T(8,128)(2,1)}, u32[]{:S(2)}) copy-start(bf16[512,1024]{1,0:T(8,128)(2,1)} %spread_panels.3) | copy-start | bytes 3145732
  87.3 15.6 %all-to-all-start.2 = ((bf16[4,512,256]{2,1,0:T(8,128)(2,1)}), bf16[4,512,256]{2,1,0:T(8,128)(2,1)S(1)}, u32[]{:S(2)}, u32[]{:S(2)}) async-start(bf16[4,512,256]{2,1,0:T(8,128)(2,1)} %broadcast_in_dim.48), calls=%async_computation.2 | async-start | bytes 2097152 | tf_op jit(solution)/shard_map/separators/all_to_all | solution.py:23
  103.5 21.5 %copy-start.7 = (s32[1,32]{1,0:T(1,128)S(1)}, s32[1,32]{1,0:T(1,128)}, u32[]{:S(2)}) copy-start(s32[1,32]{1,0:T(1,128)} %param.14) | copy-start | bytes 388
  121.4 16.7 %all-to-all-start.4 = ((bf16[8,128,256]{2,1,0:T(8,128)(2,1)}), bf16[8,128,256]{2,1,0:T(8,128)(2,1)S(1)}, u32[]{:S(2)}, u32[]{:S(2)}) async-start(bf16[8,128,256]{2,1,0:T(8,128)(2,1)} %broadcast_in_dim.50), calls=%async_computation.4 | async-start | bytes 1048576 | tf_op jit(solution)/shard_map/spread_solution/all_to_all | solution.py:23
  138.1 25.1 %all-to-all-start.5 = ((bf16[8,128,256]{2,1,0:T(8,128)(2,1)}), bf16[8,128,256]{2,1,0:T(8,128)(2,1)}, u32[]{:S(2)}, u32[]{:S(2)}) async-start(bf16[8,128,256]{2,1,0:T(8,128)(2,1)} %select_reduce_fusion), calls=%async_computation.5 | async-start | bytes 1048576 | tf_op jit(solution)/shard_map/order_rows/all_to_all | solution.py:23
  142.3 13.3 %collective-permute-start.10 = (bf16[8,128,256]{2,1,0:T(8,128)(2,1)S(1)}, bf16[8,128,256]{2,1,0:T(8,128)(2,1)S(1)}, u32[]{:S(2)}, u32[]{:S(2)}) collective-permute-start(bf16[8,128,256]{2,1,0:T(8,128)(2,1)S(1)} %all-to-all-done.4), channel_id=1, source_target_pairs={{0,1},{1,2},{2,3},{3,0},{4,5},{5,6},{6,7},{7,4},{8,9},{9,10},{10,1... | collective-permute-start | bytes 1572872 | tf_op jit(solution)/shard_map/spread_solution/ppermute | solution.py:197
  143.0 12.7 %collective-permute-start.9 = (bf16[8,128,256]{2,1,0:T(8,128)(2,1)S(1)}, bf16[8,128,256]{2,1,0:T(8,128)(2,1)S(1)}, u32[]{:S(2)}, u32[]{:S(2)}) collective-permute-start(bf16[8,128,256]{2,1,0:T(8,128)(2,1)S(1)} %all-to-all-done.4), channel_id=1, source_target_pairs={{0,3},{1,0},{2,1},{3,2},{4,7},{5,4},{6,5},{7,6},{8,11},{9,8},{10,9... | collective-permute-start | bytes 1572872 | tf_op jit(solution)/shard_map/spread_solution/ppermute | solution.py:197
  155.6 7.7 %collective-permute-start.11 = (bf16[4,128,256]{2,1,0:T(8,128)(2,1)S(1)}, bf16[4,128,256]{2,1,0:T(8,128)(2,1)S(1)}, u32[]{:S(2)}, u32[]{:S(2)}) collective-permute-start(bf16[4,128,256]{2,1,0:T(8,128)(2,1)S(1)} %slice.59), channel_id=1, source_target_pairs={{0,1},{1,2},{2,3},{3,0},{4,5},{5,6},{6,7},{7,4},{8,9},{9,10},{10,1... | collective-permute-start | bytes 786440 | tf_op jit(solution)/shard_map/spread_solution/ppermute | solution.py:197
  155.7 7.5 %collective-permute-start.12 = (bf16[4,128,256]{2,1,0:T(8,128)(2,1)S(1)}, bf16[4,128,256]{2,1,0:T(8,128)(2,1)}, u32[]{:S(2)}, u32[]{:S(2)}) collective-permute-start(bf16[4,128,256]{2,1,0:T(8,128)(2,1)S(1)} %slice.60), channel_id=1, source_target_pairs={{0,3},{1,0},{2,1},{3,2},{4,7},{5,4},{6,5},{7,6},{8,11},{9,8},{10,9... | collective-permute-start | bytes 786440 | tf_op jit(solution)/shard_map/spread_solution/ppermute | solution.py:197
  164.3 7.9 %collective-permute-start.13 = (bf16[32,128,256]{2,1,0:T(8,128)(2,1)S(1)}, bf16[32,128,256]{2,1,0:T(8,128)(2,1)}, u32[]{:S(2)}, u32[]{:S(2)}) collective-permute-start(bf16[32,128,256]{2,1,0:T(8,128)(2,1)S(1)} %constant_dynamic-update-slice_fusion.refs_5_), channel_id=1, source_target_pairs={{0,32},{32,0},{64,96},{96,64},{128,160},{160,128},{192,224},{224,1... | collective-permute-start | bytes 6291464 | tf_op jit(solution)/shard_map/leaf_backward/ppermute | solution.py:28
  167.2 5.1 %copy-start = (s32[32,5]{0,1:T(8,128)S(1)}, s32[32,5]{0,1:T(8,128)}, u32[]{:S(2)}) copy-start(s32[32,5]{0,1:T(8,128)} %param.11) | copy-start | bytes 1924
  167.2 5.0 %copy-start.1 = (s32[32]{0:T(128)S(1)}, s32[32]{0:T(128)}, u32[]{:S(2)}) copy-start(s32[32]{0:T(128)} %refs_1_.2) | copy-start | bytes 388

commit v3 on v2

--- a/solution.py
+++ b/solution.py
@@ -110,30 +110,40 @@
     )(block_rows.T, fill_count, leaf_inverse, leaf_rhs, off_blocks)
 
 
-def hold_kernel(per, *refs):
-    count = len(refs) // 2
-    sems = refs[-1]
+def hold_kernel(per, order_ref, blocks, *refs):
+    count = (len(refs) - 3) // 2
+    rows_out, sems, row_sem = refs[-3:]
     copies = []
     for i, (source, target) in enumerate(zip(refs[:count], refs[count:])):
         for chunk in range(source.shape[0] // per):
             some = pl.ds(chunk * per, per)
             copies.append(pltpu.make_async_copy(source.at[some], target.at[some], sems.at[i, chunk]))
             copies[-1].start()
+    me = lax.axis_index("front")
+    holder = jnp.int32(0)
+    for slot in range(order_ref.shape[1]):
+        holder = jnp.where(order_ref[0, slot] == me, slot // X, holder)
+    copies.append(pltpu.make_async_copy(blocks.at[pl.ds(holder, 1)], rows_out, row_sem))
+    copies[-1].start()
     for copy in copies:
         copy.wait()
 
 
-def hold(*values, per=8):
+def hold(order, blocks, *values, per=8):
     anywhere = pl.BlockSpec(memory_space=pl.ANY)
     near_by = pl.BlockSpec(memory_space=pltpu.VMEM)
     return pl.pallas_call(
         functools.partial(hold_kernel, per),
-        in_specs=[anywhere] * len(values),
-        out_specs=[near_by] * len(values),
-        out_shape=[pltpu.VMEM(value.shape, value.dtype) for value in values],
-        scratch_shapes=[pltpu.SemaphoreType.DMA((len(values), values[0].shape[0] // per))],
+        in_specs=[pl.BlockSpec(memory_space=pltpu.SMEM)] + [anywhere] * (1 + len(values)),
+        out_specs=[near_by] * len(values) + [anywhere],
+        out_shape=[pltpu.VMEM(value.shape, value.dtype) for value in values]
+        + [jax.ShapeDtypeStruct((1, *blocks.shape[1:]), blocks.dtype)],
+        scratch_shapes=[
+            pltpu.SemaphoreType.DMA((len(values), values[0].shape[0] // per)),
+            pltpu.SemaphoreType.DMA,
+        ],
         compiler_params=pltpu.CompilerParams(vmem_limit_bytes=48 << 20),
-    )(*values)
+    )(order, blocks, *values)
 
 
 def backward_kernel(per, seps, starts, *refs):
@@ -293,20 +303,19 @@
     with jax.named_scope("spread_solution"):
         solved = sep_solution.astype(BF16)
         column = exchange(jnp.broadcast_to(solved[None], (rows, b, r)), along_z)
-        slot = jnp.argmax(panel_order[0] == me).astype(jnp.int32)
-        column, blocks, slot = together((column, blocks, slot))
+        column, blocks = together((column, blocks))
         behind, ahead = shift(column, 1), shift(column, -1)
         far_low, far_high = shift(behind[:half], 1), shift(ahead[half:], -1)
     with jax.named_scope("order_rows"):
         blocks = exchange(blocks, along_z)
         far_low, far_high, blocks = together((far_low, far_high, blocks))
-        sep_forward = lax.dynamic_slice_in_dim(blocks, slot // X, 1)
     with jax.named_scope("leaf_backward"):
         field = jnp.concatenate([column, ahead, far_low, far_high, behind])
         field, *leaves = together((field, forward, leaf_inverse, off_blocks))
         other = sibling(field)
+        *leaves, sep_forward = hold(panel_order, blocks, *leaves)
         leaf_solution = backward_leaves(
-            block_rows, fill_count, *hold(*leaves), [0, seps], [field, other], seps
+            block_rows, fill_count, *leaves, [0, seps], [field, other], seps
         )
     return leaf_solution, sep_forward, sep_solution[None]
 

time: 181 us -> 176 us (0.972)
  between operations: 3.83 us -> 1.11 us
  transfers between devices with their start and end apart: 19 -> 19, of which waited for: 11 -> 11; matrix products, arithmetic and copies ran while one was open for 2% -> 1% of each run, Pallas kernels for 5% -> 5%
where the time goes in v3:
time: 176 us; the launch traced here: 174 us
  waiting for transfers between devices  78.5 us (45%)
  starting transfers between devices  40.8 us (23%)
  Pallas kernels  22.6 us (13%)
  blocking collectives  16.4 us (9%)
  local copies, waits for them, and re-layouts  6.05 us (3%)
  other arithmetic  5.97 us (3%)
  matrix products  2.1 us (1%)
    ppermute x11, waiting for transfers between devices, shifted(): lax.ppermute(value, 'front', [(i, i // X * X + (i + by) % X) for i in ran...  40.5 us
    all_to_all x5, waiting for transfers between devices, exchange(): lax.all_to_all(value, 'front', 0, 0, tiled=True, axis_index_groups=where)  36.1 us
    all_to_all x5, starting transfers between devices, exchange(): lax.all_to_all(value, 'front', 0, 0, tiled=True, axis_index_groups=where)  22.6 us
    ppermute x11, starting transfers between devices, shifted(): lax.ppermute(value, 'front', [(i, i // X * X + (i + by) % X) for i in ran...  17.9 us
    all_to_all x1, blocking collectives, exchange(): lax.all_to_all(value, 'front', 0, 0, tiled=True, axis_index_groups=where)  16.4 us
    pallas_call x1, Pallas kernels, forward_leaves(): pl.pallas_call(functools.partial(forward_kernel, per, seps), in_specs=[sc...  8.47 us
    pallas_call x1, Pallas kernels, backward_leaves(): pl.pallas_call(functools.partial(backward_kernel, per, seps, starts), in_...  5.17 us
    pallas_call x2, Pallas kernels, local(): pl.pallas_call(kernel, in_specs=[near_by] * len(values), out_specs=[near_...  4.73 us
  transfers between devices with their start and end apart: 19, of which 11 were waited for; matrix products, arithmetic and copies ran while one was open for 1% of the time, Pallas kernels for 5%

profile of v3, /device:TPU:8, one launch (start us, length us, event | category | flops | bytes accessed | tf_op | source)
XLA Modules:
  0.0 173.5 jit_solution(15933944388011092459)
XLA Ops:
  0.6 8.5 %leaf_forward.1 = (bf16[32,128,256]{2,1,0:T(8,128)(2,1)}, bf16[8,128,256]{2,1,0:T(8,128)(2,1)S(1)}, bf16[24,128,256]{2,1,0:T(8,128)(2,1)S(1)}, bf16[8,128,256]{2,1,0:T(8,128)(2,1)S(1)}, bf16[24,128,256]{2,1,0:T(8,128)(2,1)S(1)}) custom-call(s32[5,32]{1,0:T(8,128)} %bitcast.18, s32[32]{0:T(128)} %refs_1_.2, bf16[32,128,128]{2,1,0:T(8,128)(2,1)} %refs_1_.1, ...), custom_call_target="tpu_custom_call" | custom-call | tf_op jit(solution)/shard_map/leaf_forward/pallas_call | solution.py:95
  9.1 0.1 collective-permute-start
  9.2 1.9 %collective-permute-done = bf16[8,128,256]{2,1,0:T(8,128)(2,1)S(1)} collective-permute-done((bf16[8,128,256]{2,1,0:T(8,128)(2,1)S(1)}, bf16[8,128,256]{2,1,0:T(8,128)(2,1)S(1)}, u32[]{:S(2)}, u32[]{:S(2)}) %collective-permute-start) | collective-permute-done | bytes 524320 | tf_op jit(solution)/shard_map/sum_terms/ppermute | solution.py:28
  11.1 0.1 collective-permute-start.1
  11.2 0.1 add_convert_fusion.5
  11.4 1.6 collective-permute-start.2
  13.0 1.7 collective-permute-start.4
  14.7 6.5 %collective-permute-done.2 = bf16[4,128,256]{2,1,0:T(8,128)(2,1)S(1)} collective-permute-done((bf16[4,128,256]{2,1,0:T(8,128)(2,1)S(1)}, bf16[4,128,256]{2,1,0:T(8,128)(2,1)S(1)}, u32[]{:S(2)}, u32[]{:S(2)}) %collective-permute-start.2) | collective-permute-done | bytes 262176 | tf_op jit(solution)/shard_map/sum_terms/ppermute | solution.py:207
  21.2 0.0 collective-permute-done.4
  21.3 0.0 collective-permute-done.1
  21.3 1.4 add_convert_fusion.2
  22.6 1.5 collective-permute-start.3
  24.1 1.8 %collective-permute-start.5 = (bf16[8,128,256]{2,1,0:T(8,128)(2,1)}, bf16[8,128,256]{2,1,0:T(8,128)(2,1)}, u32[]{:S(2)}, u32[]{:S(2)}) collective-permute-start(bf16[8,128,256]{2,1,0:T(8,128)(2,1)} %get-tuple-element.72), channel_id=1, source_target_pairs={{0,3},{1,0},{2,1},{3,2},{4,7},{5,4},{6,5},{7,6},{8,11},{9,8},{10,9... | collective-permute-start | bytes 1572872 | tf_op jit(solution)/shard_map/sum_terms/ppermute | solution.py:207
  25.9 2.5 %spread_panels.2 = (bf16[128,1024]{1,0:T(8,128)(2,1)}, bf16[128,1024]{1,0:T(8,128)(2,1)}, bf16[128,1024]{1,0:T(8,128)(2,1)}, bf16[128,1024]{1,0:T(8,128)(2,1)}) custom-call(bf16[1,128,4096]{2,1,0:T(8,128)(2,1)} %panel_ref), custom_call_target="tpu_custom_call" | custom-call | tf_op jit(solution)/shard_map/spread_panels/pallas_call | solution.py:216
  28.4 9.2 %collective-permute-done.3 = bf16[8,128,256]{2,1,0:T(8,128)(2,1)} collective-permute-done((bf16[8,128,256]{2,1,0:T(8,128)(2,1)}, bf16[8,128,256]{2,1,0:T(8,128)(2,1)}, u32[]{:S(2)}, u32[]{:S(2)}) %collective-permute-start.3) | collective-permute-done | bytes 524320 | tf_op jit(solution)/shard_map/sum_terms/ppermute | solution.py:207
  37.5 0.0 collective-permute-done.5
  37.5 2.3 %add_convert_fusion = bf16[8,128,256]{2,1,0:T(8,128)(2,1)} fusion(bf16[8,128,256]{2,1,0:T(8,128)(2,1)} %collective-permute-done.5, bf16[8,128,256]{2,1,0:T(8,128)(2,1)} %collective-permute-done.3, bf16[24,128,256]{2,1,0:T(8,128)(2,1)S(1)} %collective-permute-done.1, bf16[24,128,256]{2,1,0:T(8,128)(2,1)S(1)} %get-tuple-element.42), kind=kLoop, calls=%fused_computation.3 | loop fusion | flops 2097152 | bytes 2621440 | tf_op jit(solution)/shard_map/sum_terms/convert_element_type | solution.py:275
  39.8 8.6 %all-to-all-start = ((bf16[8,128,256]{2,1,0:T(8,128)(2,1)}), bf16[8,128,256]{2,1,0:T(8,128)(2,1)S(1)}, u32[]{:S(2)}, u32[]{:S(2)}) async-start(bf16[8,128,256]{2,1,0:T(8,128)(2,1)} %add_convert_fusion), calls=%async_computation | async-start | bytes 1048576 | tf_op jit(solution)/shard_map/sum_terms/all_to_all | solution.py:23
  48.4 0.9 collective-permute-start.6
  49.3 2.3 %collective-permute-start.7 = (bf16[128,1024]{1,0:T(8,128)(2,1)S(1)}, bf16[128,1024]{1,0:T(8,128)(2,1)S(1)}, u32[]{:S(2)}, u32[]{:S(2)}) collective-permute-start(bf16[128,1024]{1,0:T(8,128)(2,1)S(1)} %copy-done.12), channel_id=1, source_target_pairs={{0,3},{1,0},{2,1},{3,2},{4,7},{5,4},{6,5},{7,6},{8,11},{9,8},{10,9... | collective-permute-start | bytes 786440 | tf_op jit(solution)/shard_map/spread_panels/ppermute | solution.py:207
  51.6 4.7 %collective-permute-done.6.p1 = bf16[128,1024]{1,0:T(8,128)(2,1)S(1)} collective-permute-done((bf16[128,1024]{1,0:T(8,128)(2,1)}, bf16[128,1024]{1,0:T(8,128)(2,1)S(1)}, u32[]{:S(2)}, u32[]{:S(2)}) %collective-permute-start.6) | collective-permute-done | bytes 262176 | tf_op jit(solution)/shard_map/spread_panels/ppermute | solution.py:207
  56.4 0.0 collective-permute-done.7.p3
  56.4 8.3 %all-to-all-done = bf16[8,128,256]{2,1,0:T(8,128)(2,1)S(1)} async-done(((bf16[8,128,256]{2,1,0:T(8,128)(2,1)}), bf16[8,128,256]{2,1,0:T(8,128)(2,1)S(1)}, u32[]{:S(2)}, u32[]{:S(2)}) %all-to-all-start) | async-done | bytes 524320 | tf_op jit(solution)/shard_map/sum_terms/all_to_all | solution.py:23
  64.7 0.1 fusion.1
  64.8 0.8 broadcast_in_dim.47
  65.6 3.5 %all-to-all-start.1 = ((bf16[8,128,256]{2,1,0:T(8,128)(2,1)}), bf16[8,128,256]{2,1,0:T(8,128)(2,1)S(1)}, u32[]{:S(2)}, u32[]{:S(2)}) async-start(bf16[8,128,256]{2,1,0:T(8,128)(2,1)} %broadcast_in_dim.47), calls=%async_computation.1 | async-start | bytes 1048576 | tf_op jit(solution)/shard_map/separators/all_to_all | solution.py:23
  69.1 2.1 %collective-permute-start.8 = (bf16[128,1024]{1,0:T(8,128)(2,1)S(1)}, bf16[128,1024]{1,0:T(8,128)(2,1)S(1)}, u32[]{:S(2)}, u32[]{:S(2)}) collective-permute-start(bf16[128,1024]{1,0:T(8,128)(2,1)S(1)} %copy-done.11), channel_id=1, source_target_pairs={{0,2},{1,3},{2,0},{3,1},{4,6},{5,7},{6,4},{7,5},{8,10},{9,11},{10,... | collective-permute-start | bytes 786440 | tf_op jit(solution)/shard_map/spread_panels/ppermute | solution.py:207
  71.2 5.9 %collective-permute-done.8.p2 = bf16[128,1024]{1,0:T(8,128)(2,1)S(1)} collective-permute-done((bf16[128,1024]{1,0:T(8,128)(2,1)S(1)}, bf16[128,1024]{1,0:T(8,128)(2,1)S(1)}, u32[]{:S(2)}, u32[]{:S(2)}) %collective-permute-start.8) | collective-permute-done | bytes 262176 | tf_op jit(solution)/shard_map/spread_panels/ppermute | solution.py:207
  77.1 0.7 copy-done.8
  77.8 2.2 %spread_panels.3 = bf16[512,1024]{1,0:T(8,128)(2,1)} custom-call(bf16[128,1024]{1,0:T(8,128)(2,1)} %get-tuple-element.50.p0, bf16[128,1024]{1,0:T(8,128)(2,1)} %copy-done.6, bf16[128,1024]{1,0:T(8,128)(2,1)} %copy-done.8, bf16[128,1024]{1,0:T(8,128)(2,1)} %copy-done.7), custom_call_target="tpu_custom_call" | custom-call | tf_op jit(solution)/shard_map/spread_panels/pallas_call | solution.py:216
  80.0 4.5 %all-to-all-done.1 = bf16[8,128,256]{2,1,0:T(8,128)(2,1)S(1)} async-done(((bf16[8,128,256]{2,1,0:T(8,128)(2,1)}), bf16[8,128,256]{2,1,0:T(8,128)(2,1)S(1)}, u32[]{:S(2)}, u32[]{:S(2)}) %all-to-all-start.1) | async-done | bytes 524320 | tf_op jit(solution)/shard_map/separators/all_to_all | solution.py:23
  84.6 1.7 convolution_convert_fusion.1
  86.2 1.0 broadcast_in_dim.48
  87.3 3.5 %all-to-all-start.2 = ((bf16[4,512,256]{2,1,0:T(8,128)(2,1)}), bf16[4,512,256]{2,1,0:T(8,128)(2,1)S(1)}, u32[]{:S(2)}, u32[]{:S(2)}) async-start(bf16[4,512,256]{2,1,0:T(8,128)(2,1)} %broadcast_in_dim.48), calls=%async_computation.2 | async-start | bytes 2097152 | tf_op jit(solution)/shard_map/separators/all_to_all | solution.py:23
  90.8 0.5 copy.13
  91.4 11.5 %all-to-all-done.2 = bf16[4,512,256]{2,1,0:T(8,128)(2,1)S(1)} async-done(((bf16[4,512,256]{2,1,0:T(8,128)(2,1)}), bf16[4,512,256]{2,1,0:T(8,128)(2,1)S(1)}, u32[]{:S(2)}, u32[]{:S(2)}) %all-to-all-start.2) | async-done | bytes 1048608 | tf_op jit(solution)/shard_map/separators/all_to_all | solution.py:23
  102.9 0.1 add_convert_fusion.3
  103.0 0.4 convolution_convert_fusion
  103.5 0.0 copy-start.10
  103.5 16.4 %all_to_all.31 = bf16[8,128,256]{2,1,0:T(8,128)(2,1)S(1)} all-to-all(bf16[8,128,256]{2,1,0:T(8,128)(2,1)S(1)} %convolution_convert_fusion), channel_id=1, replica_groups={{0,4,8,12,16,20,24,28},{1,5,9,13,17,21,25,29},{2,6,10,14,18,22,26,30},{..., dimensions={0} | all-to-all | bytes 1048576 | tf_op jit(solution)/shard_map/separators/all_to_all | solution.py:23
  119.8 0.7 convert_bitcast_fusion
  120.6 0.8 broadcast_in_dim.50
  121.4 3.5 %all-to-all-start.4 = ((bf16[8,128,256]{2,1,0:T(8,128)(2,1)}), bf16[8,128,256]{2,1,0:T(8,128)(2,1)S(1)}, u32[]{:S(2)}, u32[]{:S(2)}) async-start(bf16[8,128,256]{2,1,0:T(8,128)(2,1)} %broadcast_in_dim.50), calls=%async_computation.4 | async-start | bytes 1048576 | tf_op jit(solution)/shard_map/spread_solution/all_to_all | solution.py:23
  124.9 0.1 dynamic-slice_bitcast_fusion
  125.0 0.1 broadcast_compare_fusion
  125.1 1.2 select_reduce_fusion
  126.3 11.8 %all-to-all-done.4 = bf16[8,128,256]{2,1,0:T(8,128)(2,1)S(1)} async-done(((bf16[8,128,256]{2,1,0:T(8,128)(2,1)}), bf16[8,128,256]{2,1,0:T(8,128)(2,1)S(1)}, u32[]{:S(2)}, u32[]{:S(2)}) %all-to-all-start.4) | async-done | bytes 524320 | tf_op jit(solution)/shard_map/spread_solution/all_to_all | solution.py:23
  138.1 3.5 %all-to-all-start.5 = ((bf16[8,128,256]{2,1,0:T(8,128)(2,1)}), bf16[8,128,256]{2,1,0:T(8,128)(2,1)S(1)}, u32[]{:S(2)}, u32[]{:S(2)}) async-start(bf16[8,128,256]{2,1,0:T(8,128)(2,1)} %select_reduce_fusion), calls=%async_computation.5 | async-start | bytes 1048576 | tf_op jit(solution)/shard_map/order_rows/all_to_all | solution.py:23
  141.6 0.6 collective-permute-start.9
  142.2 2.7 %collective-permute-start.11 = (bf16[8,128,256]{2,1,0:T(8,128)(2,1)S(1)}, bf16[8,128,256]{2,1,0:T(8,128)(2,1)S(1)}, u32[]{:S(2)}, u32[]{:S(2)}) collective-permute-start(bf16[8,128,256]{2,1,0:T(8,128)(2,1)S(1)} %all-to-all-done.4), channel_id=1, source_target_pairs={{0,3},{1,0},{2,1},{3,2},{4,7},{5,4},{6,5},{7,6},{8,11},{9,8},{10,9... | collective-permute-start | bytes 1572872 | tf_op jit(solution)/shard_map/spread_solution/ppermute | solution.py:207
  144.9 10.0 %collective-permute-done.9 = bf16[8,128,256]{2,1,0:T(8,128)(2,1)S(1)} collective-permute-done((bf16[8,128,256]{2,1,0:T(8,128)(2,1)S(1)}, bf16[8,128,256]{2,1,0:T(8,128)(2,1)S(1)}, u32[]{:S(2)}, u32[]{:S(2)}) %collective-permute-start.9) | collective-permute-done | bytes 524320 | tf_op jit(solution)/shard_map/spread_solution/ppermute | solution.py:207
  154.9 0.1 collective-permute-start.10
  155.0 0.0 collective-permute-done.11
  155.0 0.6 copy-done.4
  155.7 2.7 %collective-permute-start.12 = (bf16[4,128,256]{2,1,0:T(8,128)(2,1)S(1)}, bf16[4,128,256]{2,1,0:T(8,128)(2,1)}, u32[]{:S(2)}, u32[]{:S(2)}) collective-permute-start(bf16[4,128,256]{2,1,0:T(8,128)(2,1)S(1)} %slice.60), channel_id=1, source_target_pairs={{0,3},{1,0},{2,1},{3,2},{4,7},{5,4},{6,5},{7,6},{8,11},{9,8},{10,9... | collective-permute-start | bytes 786440 | tf_op jit(solution)/shard_map/spread_solution/ppermute | solution.py:207
  158.4 4.1 %collective-permute-done.10 = bf16[4,128,256]{2,1,0:T(8,128)(2,1)S(1)} collective-permute-done((bf16[4,128,256]{2,1,0:T(8,128)(2,1)S(1)}, bf16[4,128,256]{2,1,0:T(8,128)(2,1)S(1)}, u32[]{:S(2)}, u32[]{:S(2)}) %collective-permute-start.10) | collective-permute-done | bytes 262176 | tf_op jit(solution)/shard_map/spread_solution/ppermute | solution.py:207
  162.6 0.0 collective-permute-done.12
  162.6 0.0 all-to-all-done.5.blocks
  162.6 1.1 constant_dynamic-update-slice_fusion.1
  163.8 0.0 copy-start
  163.8 0.0 copy-start.1
  163.8 0.1 collective-permute-start.13
  163.9 4.2 %leaf_backward.2 = (bf16[32,128,256]{2,1,0:T(8,128)(2,1)S(1)}, bf16[32,128,128]{2,1,0:T(8,128)(2,1)S(1)}, bf16[32,5,128,128]{3,2,1,0:T(8,128)(2,1)S(1)}, bf16[1,128,256]{2,1,0:T(8,128)(2,1)}) custom-call(s32[1,32]{1,0:T(1,128)} %order_ref.1, bf16[8,128,256]{2,1,0:T(8,128)(2,1)} %copy-done.3, bf16[32,128,256]{2,1,0:T(8,128)(2,1)} %get-tuple-element.61.refs_0_, ...), custom_call_target="tpu_custom_call" | custom-call | tf_op jit(solution)/shard_map/leaf_backward/pallas_call | solution.py:135
  168.2 5.2 %leaf_backward.3 = bf16[32,128,256]{2,1,0:T(8,128)(2,1)} custom-call(s32[5,32]{1,0:T(8,128)S(1)} %bitcast.19, s32[32]{0:T(128)S(1)} %copy-done.1, bf16[32,128,256]{2,1,0:T(8,128)(2,1)S(1)} %get-tuple-element.64.refs_2_, bf16[32,128,128]{2,1,0:T(8,128)(2,1)S(1)} %get-tuple-element.65.refs_3_, bf16[32,5,128,128]{3,2,1,0:T(8,128)(2,1)S(1)} %get-tuple-element.66.refs_4_, ...), custom_call_target="tpu_custom_call" | custom-call | tf_op jit(solution)/shard_map/leaf_backward/pallas_call | solution.py:191
  (29 shorter events, 0.2 us)
Async XLA Ops:
  9.1 2.0 %collective-permute-start = (bf16[8,128,256]{2,1,0:T(8,128)(2,1)S(1)}, bf16[8,128,256]{2,1,0:T(8,128)(2,1)S(1)}, u32[]{:S(2)}, u32[]{:S(2)}) collective-permute-start(bf16[8,128,256]{2,1,0:T(8,128)(2,1)S(1)} %get-tuple-element.36), channel_id=1, source_target_pairs={{0,32},{32,0},{64,96},{96,64},{128,160},{160,128},{192,224},{224,1... | collective-permute-start | bytes 1572872 | tf_op jit(solution)/shard_map/sum_terms/ppermute | solution.py:28
  11.1 10.2 %collective-permute-start.1 = (bf16[24,128,256]{2,1,0:T(8,128)(2,1)S(1)}, bf16[24,128,256]{2,1,0:T(8,128)(2,1)S(1)}, u32[]{:S(2)}, u32[]{:S(2)}) collective-permute-start(bf16[24,128,256]{2,1,0:T(8,128)(2,1)S(1)} %get-tuple-element.43), channel_id=1, source_target_pairs={{0,32},{32,0},{64,96},{96,64},{128,160},{160,128},{192,224},{224,1... | collective-permute-start | bytes 4718600 | tf_op jit(solution)/shard_map/sum_terms/ppermute | solution.py:28
  11.4 9.9 %collective-permute-start.2 = (bf16[4,128,256]{2,1,0:T(8,128)(2,1)S(1)}, bf16[4,128,256]{2,1,0:T(8,128)(2,1)S(1)}, u32[]{:S(2)}, u32[]{:S(2)}) collective-permute-start(bf16[4,128,256]{2,1,0:T(8,128)(2,1)S(1)} %get-tuple-element.73), channel_id=1, source_target_pairs={{0,1},{1,2},{2,3},{3,0},{4,5},{5,6},{6,7},{7,4},{8,9},{9,10},{10,1... | collective-permute-start | bytes 786440 | tf_op jit(solution)/shard_map/sum_terms/ppermute | solution.py:207
  13.0 8.3 %collective-permute-start.4 = (bf16[4,128,256]{2,1,0:T(8,128)(2,1)S(1)}, bf16[4,128,256]{2,1,0:T(8,128)(2,1)S(1)}, u32[]{:S(2)}, u32[]{:S(2)}) collective-permute-start(bf16[4,128,256]{2,1,0:T(8,128)(2,1)S(1)} %get-tuple-element.74), channel_id=1, source_target_pairs={{0,3},{1,0},{2,1},{3,2},{4,7},{5,4},{6,5},{7,6},{8,11},{9,8},{10,9... | collective-permute-start | bytes 786440 | tf_op jit(solution)/shard_map/sum_terms/ppermute | solution.py:207
  22.6 14.9 %collective-permute-start.3 = (bf16[8,128,256]{2,1,0:T(8,128)(2,1)}, bf16[8,128,256]{2,1,0:T(8,128)(2,1)}, u32[]{:S(2)}, u32[]{:S(2)}) collective-permute-start(bf16[8,128,256]{2,1,0:T(8,128)(2,1)} %get-tuple-element.71), channel_id=1, source_target_pairs={{0,1},{1,2},{2,3},{3,0},{4,5},{5,6},{6,7},{7,4},{8,9},{9,10},{10,1... | collective-permute-start | bytes 1572872 | tf_op jit(solution)/shard_map/sum_terms/ppermute | solution.py:207
  24.1 13.4 %collective-permute-start.5 = (bf16[8,128,256]{2,1,0:T(8,128)(2,1)}, bf16[8,128,256]{2,1,0:T(8,128)(2,1)}, u32[]{:S(2)}, u32[]{:S(2)}) collective-permute-start(bf16[8,128,256]{2,1,0:T(8,128)(2,1)} %get-tuple-element.72), channel_id=1, source_target_pairs={{0,3},{1,0},{2,1},{3,2},{4,7},{5,4},{6,5},{7,6},{8,11},{9,8},{10,9... | collective-permute-start | bytes 1572872 | tf_op jit(solution)/shard_map/sum_terms/ppermute | solution.py:207
  28.4 20.9 %copy-start.12 = (bf16[128,1024]{1,0:T(8,128)(2,1)S(1)}, bf16[128,1024]{1,0:T(8,128)(2,1)}, u32[]{:S(2)}) copy-start(bf16[128,1024]{1,0:T(8,128)(2,1)} %get-tuple-element.49) | copy-start | bytes 786436
  28.4 36.3 %copy-start.9 = (bf16[1,128,256]{2,1,0:T(8,128)(2,1)S(1)}, bf16[1,128,256]{2,1,0:T(8,128)(2,1)}, u32[]{:S(2)}) copy-start(bf16[1,128,256]{2,1,0:T(8,128)(2,1)} %param.13) | copy-start | bytes 196612
  39.8 29.3 %copy-start.11 = (bf16[128,1024]{1,0:T(8,128)(2,1)S(1)}, bf16[128,1024]{1,0:T(8,128)(2,1)}, u32[]{:S(2)}) copy-start(bf16[128,1024]{1,0:T(8,128)(2,1)} %get-tuple-element.52) | copy-start | bytes 786436
  39.8 24.9 %all-to-all-start = ((bf16[8,128,256]{2,1,0:T(8,128)(2,1)}), bf16[8,128,256]{2,1,0:T(8,128)(2,1)S(1)}, u32[]{:S(2)}, u32[]{:S(2)}) async-start(bf16[8,128,256]{2,1,0:T(8,128)(2,1)} %add_convert_fusion), calls=%async_computation | async-start | bytes 1048576 | tf_op jit(solution)/shard_map/sum_terms/all_to_all | solution.py:23
  48.4 8.0 %collective-permute-start.6 = (bf16[128,1024]{1,0:T(8,128)(2,1)}, bf16[128,1024]{1,0:T(8,128)(2,1)S(1)}, u32[]{:S(2)}, u32[]{:S(2)}) collective-permute-start(bf16[128,1024]{1,0:T(8,128)(2,1)} %get-tuple-element.47), channel_id=1, source_target_pairs={{0,1},{1,2},{2,3},{3,0},{4,5},{5,6},{6,7},{7,4},{8,9},{9,10},{10,1... | collective-permute-start | bytes 786440 | tf_op jit(solution)/shard_map/spread_panels/ppermute | solution.py:207
  49.3 7.1 %collective-permute-start.7 = (bf16[128,1024]{1,0:T(8,128)(2,1)S(1)}, bf16[128,1024]{1,0:T(8,128)(2,1)S(1)}, u32[]{:S(2)}, u32[]{:S(2)}) collective-permute-start(bf16[128,1024]{1,0:T(8,128)(2,1)S(1)} %copy-done.12), channel_id=1, source_target_pairs={{0,3},{1,0},{2,1},{3,2},{4,7},{5,4},{6,5},{7,6},{8,11},{9,8},{10,9... | collective-permute-start | bytes 786440 | tf_op jit(solution)/shard_map/spread_panels/ppermute | solution.py:207
  56.4 20.7 %copy-start.6 = (bf16[128,1024]{1,0:T(8,128)(2,1)}, bf16[128,1024]{1,0:T(8,128)(2,1)S(1)}, u32[]{:S(2)}) copy-start(bf16[128,1024]{1,0:T(8,128)(2,1)S(1)} %collective-permute-done.6.p1) | copy-start | bytes 786436
  56.4 20.7 %copy-start.7 = (bf16[128,1024]{1,0:T(8,128)(2,1)}, bf16[128,1024]{1,0:T(8,128)(2,1)S(1)}, u32[]{:S(2)}) copy-start(bf16[128,1024]{1,0:T(8,128)(2,1)S(1)} %collective-permute-done.7.p3) | copy-start | bytes 786436
  65.6 19.0 %all-to-all-start.1 = ((bf16[8,128,256]{2,1,0:T(8,128)(2,1)}), bf16[8,128,256]{2,1,0:T(8,128)(2,1)S(1)}, u32[]{:S(2)}, u32[]{:S(2)}) async-start(bf16[8,128,256]{2,1,0:T(8,128)(2,1)} %broadcast_in_dim.47), calls=%async_computation.1 | async-start | bytes 1048576 | tf_op jit(solution)/shard_map/separators/all_to_all | solution.py:23
  69.1 8.0 %collective-permute-start.8 = (bf16[128,1024]{1,0:T(8,128)(2,1)S(1)}, bf16[128,1024]{1,0:T(8,128)(2,1)S(1)}, u32[]{:S(2)}, u32[]{:S(2)}) collective-permute-start(bf16[128,1024]{1,0:T(8,128)(2,1)S(1)} %copy-done.11), channel_id=1, source_target_pairs={{0,2},{1,3},{2,0},{3,1},{4,6},{5,7},{6,4},{7,5},{8,10},{9,11},{10,... | collective-permute-start | bytes 786440 | tf_op jit(solution)/shard_map/spread_panels/ppermute | solution.py:207
  77.1 0.7 copy-start.8
  86.2 4.6 %copy-start.2 = (bf16[512,1024]{1,0:T(8,128)(2,1)S(1)}, bf16[512,1024]{1,0:T(8,128)(2,1)}, u32[]{:S(2)}) copy-start(bf16[512,1024]{1,0:T(8,128)(2,1)} %spread_panels.3) | copy-start | bytes 3145732
  87.3 15.6 %all-to-all-start.2 = ((bf16[4,512,256]{2,1,0:T(8,128)(2,1)}), bf16[4,512,256]{2,1,0:T(8,128)(2,1)S(1)}, u32[]{:S(2)}, u32[]{:S(2)}) async-start(bf16[4,512,256]{2,1,0:T(8,128)(2,1)} %broadcast_in_dim.48), calls=%async_computation.2 | async-start | bytes 2097152 | tf_op jit(solution)/shard_map/separators/all_to_all | solution.py:23
  103.5 21.5 %copy-start.10 = (s32[1,32]{1,0:T(1,128)S(1)}, s32[1,32]{1,0:T(1,128)}, u32[]{:S(2)}) copy-start(s32[1,32]{1,0:T(1,128)} %order_ref.1) | copy-start | bytes 388
  121.4 16.7 %all-to-all-start.4 = ((bf16[8,128,256]{2,1,0:T(8,128)(2,1)}), bf16[8,128,256]{2,1,0:T(8,128)(2,1)S(1)}, u32[]{:S(2)}, u32[]{:S(2)}) async-start(bf16[8,128,256]{2,1,0:T(8,128)(2,1)} %broadcast_in_dim.50), calls=%async_computation.4 | async-start | bytes 1048576 | tf_op jit(solution)/shard_map/spread_solution/all_to_all | solution.py:23
  138.1 24.5 %all-to-all-start.5 = ((bf16[8,128,256]{2,1,0:T(8,128)(2,1)}), bf16[8,128,256]{2,1,0:T(8,128)(2,1)S(1)}, u32[]{:S(2)}, u32[]{:S(2)}) async-start(bf16[8,128,256]{2,1,0:T(8,128)(2,1)} %select_reduce_fusion), calls=%async_computation.5 | async-start | bytes 1048576 | tf_op jit(solution)/shard_map/order_rows/all_to_all | solution.py:23
  141.6 13.3 %collective-permute-start.9 = (bf16[8,128,256]{2,1,0:T(8,128)(2,1)S(1)}, bf16[8,128,256]{2,1,0:T(8,128)(2,1)S(1)}, u32[]{:S(2)}, u32[]{:S(2)}) collective-permute-start(bf16[8,128,256]{2,1,0:T(8,128)(2,1)S(1)} %all-to-all-done.4), channel_id=1, source_target_pairs={{0,1},{1,2},{2,3},{3,0},{4,5},{5,6},{6,7},{7,4},{8,9},{9,10},{10,1... | collective-permute-start | bytes 1572872 | tf_op jit(solution)/shard_map/spread_solution/ppermute | solution.py:207
  142.2 12.8 %collective-permute-start.11 = (bf16[8,128,256]{2,1,0:T(8,128)(2,1)S(1)}, bf16[8,128,256]{2,1,0:T(8,128)(2,1)S(1)}, u32[]{:S(2)}, u32[]{:S(2)}) collective-permute-start(bf16[8,128,256]{2,1,0:T(8,128)(2,1)S(1)} %all-to-all-done.4), channel_id=1, source_target_pairs={{0,3},{1,0},{2,1},{3,2},{4,7},{5,4},{6,5},{7,6},{8,11},{9,8},{10,9... | collective-permute-start | bytes 1572872 | tf_op jit(solution)/shard_map/spread_solution/ppermute | solution.py:207
  154.9 0.8 copy-start.4
  154.9 7.7 %collective-permute-start.10 = (bf16[4,128,256]{2,1,0:T(8,128)(2,1)S(1)}, bf16[4,128,256]{2,1,0:T(8,128)(2,1)S(1)}, u32[]{:S(2)}, u32[]{:S(2)}) collective-permute-start(bf16[4,128,256]{2,1,0:T(8,128)(2,1)S(1)} %slice.59), channel_id=1, source_target_pairs={{0,1},{1,2},{2,3},{3,0},{4,5},{5,6},{6,7},{7,4},{8,9},{9,10},{10,1... | collective-permute-start | bytes 786440 | tf_op jit(solution)/shard_map/spread_solution/ppermute | solution.py:207
  155.7 6.9 %collective-permute-start.12 = (bf16[4,128,256]{2,1,0:T(8,128)(2,1)S(1)}, bf16[4,128,256]{2,1,0:T(8,128)(2,1)}, u32[]{:S(2)}, u32[]{:S(2)}) collective-permute-start(bf16[4,128,256]{2,1,0:T(8,128)(2,1)S(1)} %slice.60), channel_id=1, source_target_pairs={{0,3},{1,0},{2,1},{3,2},{4,7},{5,4},{6,5},{7,6},{8,11},{9,8},{10,9... | collective-permute-start | bytes 786440 | tf_op jit(solution)/shard_map/spread_solution/ppermute | solution.py:207
  158.4 5.4 %copy-start.5 = (bf16[8,128,256]{2,1,0:T(8,128)(2,1)S(1)}, bf16[8,128,256]{2,1,0:T(8,128)(2,1)}, u32[]{:S(2)}) copy-start(bf16[8,128,256]{2,1,0:T(8,128)(2,1)} %copy-done.4) | copy-start | bytes 1572868
  162.6 1.4 copy-start.3
  163.8 4.4 %copy-start = (s32[32,5]{0,1:T(8,128)S(1)}, s32[32,5]{0,1:T(8,128)}, u32[]{:S(2)}) copy-start(s32[32,5]{0,1:T(8,128)} %param.11) | copy-start | bytes 1924
  163.8 4.4 %copy-start.1 = (s32[32]{0:T(128)S(1)}, s32[32]{0:T(128)}, u32[]{:S(2)}) copy-start(s32[32]{0:T(128)} %refs_1_.2) | copy-start | bytes 388
  163.8 4.3 %collective-permute-start.13 = (bf16[32,128,256]{2,1,0:T(8,128)(2,1)S(1)}, bf16[32,128,256]{2,1,0:T(8,128)(2,1)S(1)}, u32[]{:S(2)}, u32[]{:S(2)}) collective-permute-start(bf16[32,128,256]{2,1,0:T(8,128)(2,1)S(1)} %constant_dynamic-update-slice_fusion.refs_5_), channel_id=1, source_target_pairs={{0,32},{32,0},{64,96},{96,64},{128,160},{160,128},{192,224},{224,1... | collective-permute-start | bytes 6291464 | tf_op jit(solution)/shard_map/leaf_backward/ppermute | solution.py:28

commit v4 on v3

--- a/solution.py
+++ b/solution.py
@@ -289,8 +289,7 @@
         separator_in = (sep_rhs[0].astype(F32) - summed).astype(BF16)
         right = exchange(jnp.broadcast_to(separator_in[None], (rows, b, r)), along_z)
         part = jnp.dot(panel, right.reshape(rows * b, r), preferred_element_type=F32).astype(BF16)
-        parts = exchange(jnp.broadcast_to(part[None], (X, X * b, r)).reshape(X * X * b, r), along_x)
-        solved_rows = added(*parts.reshape(X, X * b, r)).astype(BF16)
+        solved_rows = added(part, *(shift(part, by) for by in (2, 1, -1))).astype(BF16)
         adjoint = lax.dot_general(panel, solved_rows, (((0,), (0,)), ((), ())), preferred_element_type=F32)
         sep_solution = added(*exchange(adjoint.reshape(rows, b, r).astype(BF16), along_z))
     with jax.named_scope("order_rows"):

time: 176 us -> 171 us (0.972)
  waiting for transfers between devices: 78.5 us -> 75.1 us
    all_to_all x5 -> x4, waiting for transfers between devices: 36.1 us -> 24.6 us  [exchange(): lax.all_to_all(value, 'front', 0, 0, tiled=True, axis_index_groups=where)]
    ppermute x11 -> x14, waiting for transfers between devices: 40.5 us -> 48.6 us  [shifted(): lax.ppermute(value, 'front', [(i, i // X * X + (i + by) % X) for i in ran...]
    ppermute x11 -> x14, starting transfers between devices: 17.9 us -> 21.6 us  [shifted(): lax.ppermute(value, 'front', [(i, i // X * X + (i + by) % X) for i in ran...]
    all_to_all x5 -> x4, starting transfers between devices: 22.6 us -> 19.1 us  [exchange(): lax.all_to_all(value, 'front', 0, 0, tiled=True, axis_index_groups=where)]
  transfers between devices with their start and end apart: 19 -> 21, of which waited for: 11 -> 13; matrix products, arithmetic and copies ran while one was open for 1% -> 1% of each run, Pallas kernels for 5% -> 5%
where the time goes in v4:
time: 171 us; the launch traced here: 169 us
  waiting for transfers between devices  75.1 us (44%)
  starting transfers between devices  41.3 us (24%)
  Pallas kernels  22.6 us (13%)
  blocking collectives  16.3 us (10%)
  other arithmetic  5.97 us (3%)
  local copies, waits for them, and re-layouts  4.42 us (3%)
  matrix products  2.15 us (1%)
    ppermute x14, waiting for transfers between devices, shifted(): lax.ppermute(value, 'front', [(i, i // X * X + (i + by) % X) for i in ran...  48.6 us
    all_to_all x4, waiting for transfers between devices, exchange(): lax.all_to_all(value, 'front', 0, 0, tiled=True, axis_index_groups=where)  24.6 us
    ppermute x14, starting transfers between devices, shifted(): lax.ppermute(value, 'front', [(i, i // X * X + (i + by) % X) for i in ran...  21.6 us
    all_to_all x4, starting transfers between devices, exchange(): lax.all_to_all(value, 'front', 0, 0, tiled=True, axis_index_groups=where)  19.1 us
    all_to_all x1, blocking collectives, exchange(): lax.all_to_all(value, 'front', 0, 0, tiled=True, axis_index_groups=where)  16.3 us
    pallas_call x1, Pallas kernels, forward_leaves(): pl.pallas_call(functools.partial(forward_kernel, per, seps), in_specs=[sc...  8.47 us
    pallas_call x1, Pallas kernels, backward_leaves(): pl.pallas_call(functools.partial(backward_kernel, per, seps, starts), in_...  5.17 us
    pallas_call x2, Pallas kernels, local(): pl.pallas_call(kernel, in_specs=[near_by] * len(values), out_specs=[near_...  4.76 us
  transfers between devices with their start and end apart: 21, of which 13 were waited for; matrix products, arithmetic and copies ran while one was open for 1% of the time, Pallas kernels for 5%

profile of v4, /device:TPU:8, one launch (start us, length us, event | category | flops | bytes accessed | tf_op | source)
XLA Modules:
  0.0 168.9 jit_solution(13071414825836066717)
XLA Ops:
  0.6 8.5 %leaf_forward.1 = (bf16[32,128,256]{2,1,0:T(8,128)(2,1)}, bf16[8,128,256]{2,1,0:T(8,128)(2,1)S(1)}, bf16[24,128,256]{2,1,0:T(8,128)(2,1)S(1)}, bf16[8,128,256]{2,1,0:T(8,128)(2,1)S(1)}, bf16[24,128,256]{2,1,0:T(8,128)(2,1)S(1)}) custom-call(s32[5,32]{1,0:T(8,128)} %bitcast.14, s32[32]{0:T(128)} %refs_1_.2, bf16[32,128,128]{2,1,0:T(8,128)(2,1)} %refs_1_.1, ...), custom_call_target="tpu_custom_call" | custom-call | tf_op jit(solution)/shard_map/leaf_forward/pallas_call | solution.py:95
  9.1 0.1 collective-permute-start
  9.2 1.9 %collective-permute-done = bf16[8,128,256]{2,1,0:T(8,128)(2,1)S(1)} collective-permute-done((bf16[8,128,256]{2,1,0:T(8,128)(2,1)S(1)}, bf16[8,128,256]{2,1,0:T(8,128)(2,1)S(1)}, u32[]{:S(2)}, u32[]{:S(2)}) %collective-permute-start) | collective-permute-done | bytes 524320 | tf_op jit(solution)/shard_map/sum_terms/ppermute | solution.py:28
  11.1 0.1 collective-permute-start.1
  11.2 0.1 add_convert_fusion.5
  11.4 1.6 collective-permute-start.2
  13.0 1.7 %collective-permute-start.4 = (bf16[4,128,256]{2,1,0:T(8,128)(2,1)S(1)}, bf16[4,128,256]{2,1,0:T(8,128)(2,1)S(1)}, u32[]{:S(2)}, u32[]{:S(2)}) collective-permute-start(bf16[4,128,256]{2,1,0:T(8,128)(2,1)S(1)} %get-tuple-element.74), channel_id=1, source_target_pairs={{0,3},{1,0},{2,1},{3,2},{4,7},{5,4},{6,5},{7,6},{8,11},{9,8},{10,9... | collective-permute-start | bytes 786440 | tf_op jit(solution)/shard_map/sum_terms/ppermute | solution.py:207
  14.7 6.5 %collective-permute-done.2 = bf16[4,128,256]{2,1,0:T(8,128)(2,1)S(1)} collective-permute-done((bf16[4,128,256]{2,1,0:T(8,128)(2,1)S(1)}, bf16[4,128,256]{2,1,0:T(8,128)(2,1)S(1)}, u32[]{:S(2)}, u32[]{:S(2)}) %collective-permute-start.2) | collective-permute-done | bytes 262176 | tf_op jit(solution)/shard_map/sum_terms/ppermute | solution.py:207
  21.2 0.0 collective-permute-done.4
  21.3 0.0 collective-permute-done.1
  21.3 1.4 add_convert_fusion.2
  22.6 1.5 collective-permute-start.3
  24.1 1.8 %collective-permute-start.5 = (bf16[8,128,256]{2,1,0:T(8,128)(2,1)}, bf16[8,128,256]{2,1,0:T(8,128)(2,1)}, u32[]{:S(2)}, u32[]{:S(2)}) collective-permute-start(bf16[8,128,256]{2,1,0:T(8,128)(2,1)} %get-tuple-element.72), channel_id=1, source_target_pairs={{0,3},{1,0},{2,1},{3,2},{4,7},{5,4},{6,5},{7,6},{8,11},{9,8},{10,9... | collective-permute-start | bytes 1572872 | tf_op jit(solution)/shard_map/sum_terms/ppermute | solution.py:207
  25.9 2.5 %spread_panels.2 = (bf16[128,1024]{1,0:T(8,128)(2,1)}, bf16[128,1024]{1,0:T(8,128)(2,1)}, bf16[128,1024]{1,0:T(8,128)(2,1)}, bf16[128,1024]{1,0:T(8,128)(2,1)}) custom-call(bf16[1,128,4096]{2,1,0:T(8,128)(2,1)} %panel_ref), custom_call_target="tpu_custom_call" | custom-call | tf_op jit(solution)/shard_map/spread_panels/pallas_call | solution.py:216
  28.4 9.2 %collective-permute-done.3 = bf16[8,128,256]{2,1,0:T(8,128)(2,1)} collective-permute-done((bf16[8,128,256]{2,1,0:T(8,128)(2,1)}, bf16[8,128,256]{2,1,0:T(8,128)(2,1)}, u32[]{:S(2)}, u32[]{:S(2)}) %collective-permute-start.3) | collective-permute-done | bytes 524320 | tf_op jit(solution)/shard_map/sum_terms/ppermute | solution.py:207
  37.5 0.0 collective-permute-done.5
  37.5 2.3 %add_convert_fusion = bf16[8,128,256]{2,1,0:T(8,128)(2,1)} fusion(bf16[8,128,256]{2,1,0:T(8,128)(2,1)} %collective-permute-done.5, bf16[8,128,256]{2,1,0:T(8,128)(2,1)} %collective-permute-done.3, bf16[24,128,256]{2,1,0:T(8,128)(2,1)S(1)} %collective-permute-done.1, bf16[24,128,256]{2,1,0:T(8,128)(2,1)S(1)} %get-tuple-element.42), kind=kLoop, calls=%fused_computation.3 | loop fusion | flops 2097152 | bytes 2621440 | tf_op jit(solution)/shard_map/sum_terms/convert_element_type | solution.py:275
  39.8 8.6 %all-to-all-start = ((bf16[8,128,256]{2,1,0:T(8,128)(2,1)}), bf16[8,128,256]{2,1,0:T(8,128)(2,1)S(1)}, u32[]{:S(2)}, u32[]{:S(2)}) async-start(bf16[8,128,256]{2,1,0:T(8,128)(2,1)} %add_convert_fusion), calls=%async_computation | async-start | bytes 1048576 | tf_op jit(solution)/shard_map/sum_terms/all_to_all | solution.py:23
  48.4 0.9 collective-permute-start.6
  49.3 2.3 %collective-permute-start.7 = (bf16[128,1024]{1,0:T(8,128)(2,1)S(1)}, bf16[128,1024]{1,0:T(8,128)(2,1)S(1)}, u32[]{:S(2)}, u32[]{:S(2)}) collective-permute-start(bf16[128,1024]{1,0:T(8,128)(2,1)S(1)} %copy-done.12), channel_id=1, source_target_pairs={{0,3},{1,0},{2,1},{3,2},{4,7},{5,4},{6,5},{7,6},{8,11},{9,8},{10,9... | collective-permute-start | bytes 786440 | tf_op jit(solution)/shard_map/spread_panels/ppermute | solution.py:207
  51.6 4.7 %collective-permute-done.6.p1 = bf16[128,1024]{1,0:T(8,128)(2,1)S(1)} collective-permute-done((bf16[128,1024]{1,0:T(8,128)(2,1)}, bf16[128,1024]{1,0:T(8,128)(2,1)S(1)}, u32[]{:S(2)}, u32[]{:S(2)}) %collective-permute-start.6) | collective-permute-done | bytes 262176 | tf_op jit(solution)/shard_map/spread_panels/ppermute | solution.py:207
  56.4 0.0 collective-permute-done.7.p3
  56.4 8.3 %all-to-all-done = bf16[8,128,256]{2,1,0:T(8,128)(2,1)S(1)} async-done(((bf16[8,128,256]{2,1,0:T(8,128)(2,1)}), bf16[8,128,256]{2,1,0:T(8,128)(2,1)S(1)}, u32[]{:S(2)}, u32[]{:S(2)}) %all-to-all-start) | async-done | bytes 524320 | tf_op jit(solution)/shard_map/sum_terms/all_to_all | solution.py:23
  64.7 0.1 fusion
  64.8 0.8 broadcast_in_dim.43
  65.6 3.5 %all-to-all-start.1 = ((bf16[8,128,256]{2,1,0:T(8,128)(2,1)}), bf16[8,128,256]{2,1,0:T(8,128)(2,1)S(1)}, u32[]{:S(2)}, u32[]{:S(2)}) async-start(bf16[8,128,256]{2,1,0:T(8,128)(2,1)} %broadcast_in_dim.43), calls=%async_computation.1 | async-start | bytes 1048576 | tf_op jit(solution)/shard_map/separators/all_to_all | solution.py:23
  69.1 2.1 %collective-permute-start.8 = (bf16[128,1024]{1,0:T(8,128)(2,1)S(1)}, bf16[128,1024]{1,0:T(8,128)(2,1)S(1)}, u32[]{:S(2)}, u32[]{:S(2)}) collective-permute-start(bf16[128,1024]{1,0:T(8,128)(2,1)S(1)} %copy-done.11), channel_id=1, source_target_pairs={{0,2},{1,3},{2,0},{3,1},{4,6},{5,7},{6,4},{7,5},{8,10},{9,11},{10,... | collective-permute-start | bytes 786440 | tf_op jit(solution)/shard_map/spread_panels/ppermute | solution.py:207
  71.2 5.9 %collective-permute-done.8.p2 = bf16[128,1024]{1,0:T(8,128)(2,1)S(1)} collective-permute-done((bf16[128,1024]{1,0:T(8,128)(2,1)S(1)}, bf16[128,1024]{1,0:T(8,128)(2,1)S(1)}, u32[]{:S(2)}, u32[]{:S(2)}) %collective-permute-start.8) | collective-permute-done | bytes 262176 | tf_op jit(solution)/shard_map/spread_panels/ppermute | solution.py:207
  77.1 0.7 copy-done.8
  77.8 2.3 %spread_panels.3 = bf16[512,1024]{1,0:T(8,128)(2,1)} custom-call(bf16[128,1024]{1,0:T(8,128)(2,1)} %get-tuple-element.50.p0, bf16[128,1024]{1,0:T(8,128)(2,1)} %copy-done.6, bf16[128,1024]{1,0:T(8,128)(2,1)} %copy-done.8, bf16[128,1024]{1,0:T(8,128)(2,1)} %copy-done.7), custom_call_target="tpu_custom_call" | custom-call | tf_op jit(solution)/shard_map/spread_panels/pallas_call | solution.py:216
  80.0 4.5 %all-to-all-done.1 = bf16[8,128,256]{2,1,0:T(8,128)(2,1)S(1)} async-done(((bf16[8,128,256]{2,1,0:T(8,128)(2,1)}), bf16[8,128,256]{2,1,0:T(8,128)(2,1)S(1)}, u32[]{:S(2)}, u32[]{:S(2)}) %all-to-all-start.1) | async-done | bytes 524320 | tf_op jit(solution)/shard_map/separators/all_to_all | solution.py:23
  84.5 1.7 convolution_convert_fusion.1
  86.2 0.1 collective-permute-start.10
  86.3 3.2 %collective-permute-start.11 = (bf16[512,256]{1,0:T(8,128)(2,1)S(1)}, bf16[512,256]{1,0:T(8,128)(2,1)S(1)}, u32[]{:S(2)}, u32[]{:S(2)}) collective-permute-start(bf16[512,256]{1,0:T(8,128)(2,1)S(1)} %convolution_convert_fusion.1), channel_id=1, source_target_pairs={{0,3},{1,0},{2,1},{3,2},{4,7},{5,4},{6,5},{7,6},{8,11},{9,8},{10,9... | collective-permute-start | bytes 786440 | tf_op jit(solution)/shard_map/separators/ppermute | solution.py:207
  89.5 0.4 collective-permute-start.9
  89.9 5.3 %collective-permute-done.10 = bf16[512,256]{1,0:T(8,128)(2,1)S(1)} collective-permute-done((bf16[512,256]{1,0:T(8,128)(2,1)S(1)}, bf16[512,256]{1,0:T(8,128)(2,1)S(1)}, u32[]{:S(2)}, u32[]{:S(2)}) %collective-permute-start.10) | collective-permute-done | bytes 262176 | tf_op jit(solution)/shard_map/separators/ppermute | solution.py:207
  95.2 1.9 %collective-permute-done.11 = bf16[512,256]{1,0:T(8,128)(2,1)S(1)} collective-permute-done((bf16[512,256]{1,0:T(8,128)(2,1)S(1)}, bf16[512,256]{1,0:T(8,128)(2,1)S(1)}, u32[]{:S(2)}, u32[]{:S(2)}) %collective-permute-start.11) | collective-permute-done | bytes 262176 | tf_op jit(solution)/shard_map/separators/ppermute | solution.py:207
  97.2 0.9 collective-permute-done.9
  98.1 0.1 add_convert_fusion.3
  98.2 0.5 convolution_convert_fusion
  98.7 0.0 copy-start.10
  98.7 16.3 %all_to_all.25 = bf16[8,128,256]{2,1,0:T(8,128)(2,1)S(1)} all-to-all(bf16[8,128,256]{2,1,0:T(8,128)(2,1)S(1)} %bitcast.18), channel_id=1, replica_groups={{0,4,8,12,16,20,24,28},{1,5,9,13,17,21,25,29},{2,6,10,14,18,22,26,30},{..., dimensions={0} | all-to-all | bytes 1048576 | tf_op jit(solution)/shard_map/separators/all_to_all | solution.py:23
  115.0 0.7 convert_bitcast_fusion
  115.7 0.8 broadcast_in_dim.45
  116.5 3.5 %all-to-all-start.3 = ((bf16[8,128,256]{2,1,0:T(8,128)(2,1)}), bf16[8,128,256]{2,1,0:T(8,128)(2,1)S(1)}, u32[]{:S(2)}, u32[]{:S(2)}) async-start(bf16[8,128,256]{2,1,0:T(8,128)(2,1)} %broadcast_in_dim.45), calls=%async_computation.3 | async-start | bytes 1048576 | tf_op jit(solution)/shard_map/spread_solution/all_to_all | solution.py:23
  120.1 0.1 dynamic-slice_bitcast_fusion
  120.2 0.1 broadcast_compare_fusion
  120.2 1.2 select_reduce_fusion
  121.4 11.8 %all-to-all-done.3 = bf16[8,128,256]{2,1,0:T(8,128)(2,1)S(1)} async-done(((bf16[8,128,256]{2,1,0:T(8,128)(2,1)}), bf16[8,128,256]{2,1,0:T(8,128)(2,1)S(1)}, u32[]{:S(2)}, u32[]{:S(2)}) %all-to-all-start.3) | async-done | bytes 524320 | tf_op jit(solution)/shard_map/spread_solution/all_to_all | solution.py:23
  133.2 3.5 %all-to-all-start.4 = ((bf16[8,128,256]{2,1,0:T(8,128)(2,1)}), bf16[8,128,256]{2,1,0:T(8,128)(2,1)S(1)}, u32[]{:S(2)}, u32[]{:S(2)}) async-start(bf16[8,128,256]{2,1,0:T(8,128)(2,1)} %select_reduce_fusion), calls=%async_computation.4 | async-start | bytes 1048576 | tf_op jit(solution)/shard_map/order_rows/all_to_all | solution.py:23
  136.7 1.0 collective-permute-start.12
  137.8 2.3 %collective-permute-start.14 = (bf16[8,128,256]{2,1,0:T(8,128)(2,1)S(1)}, bf16[8,128,256]{2,1,0:T(8,128)(2,1)S(1)}, u32[]{:S(2)}, u32[]{:S(2)}) collective-permute-start(bf16[8,128,256]{2,1,0:T(8,128)(2,1)S(1)} %all-to-all-done.3), channel_id=1, source_target_pairs={{0,3},{1,0},{2,1},{3,2},{4,7},{5,4},{6,5},{7,6},{8,11},{9,8},{10,9... | collective-permute-start | bytes 1572872 | tf_op jit(solution)/shard_map/spread_solution/ppermute | solution.py:207
  140.0 10.0 %collective-permute-done.12 = bf16[8,128,256]{2,1,0:T(8,128)(2,1)S(1)} collective-permute-done((bf16[8,128,256]{2,1,0:T(8,128)(2,1)S(1)}, bf16[8,128,256]{2,1,0:T(8,128)(2,1)S(1)}, u32[]{:S(2)}, u32[]{:S(2)}) %collective-permute-start.12) | collective-permute-done | bytes 524320 | tf_op jit(solution)/shard_map/spread_solution/ppermute | solution.py:207
  150.0 0.1 collective-permute-start.13
  150.2 0.6 copy-done.3
  150.8 2.7 %collective-permute-start.15 = (bf16[4,128,256]{2,1,0:T(8,128)(2,1)S(1)}, bf16[4,128,256]{2,1,0:T(8,128)(2,1)}, u32[]{:S(2)}, u32[]{:S(2)}) collective-permute-start(bf16[4,128,256]{2,1,0:T(8,128)(2,1)S(1)} %slice.52), channel_id=1, source_target_pairs={{0,3},{1,0},{2,1},{3,2},{4,7},{5,4},{6,5},{7,6},{8,11},{9,8},{10,9... | collective-permute-start | bytes 786440 | tf_op jit(solution)/shard_map/spread_solution/ppermute | solution.py:207
  153.6 4.1 %collective-permute-done.13 = bf16[4,128,256]{2,1,0:T(8,128)(2,1)S(1)} collective-permute-done((bf16[4,128,256]{2,1,0:T(8,128)(2,1)S(1)}, bf16[4,128,256]{2,1,0:T(8,128)(2,1)S(1)}, u32[]{:S(2)}, u32[]{:S(2)}) %collective-permute-start.13) | collective-permute-done | bytes 262176 | tf_op jit(solution)/shard_map/spread_solution/ppermute | solution.py:207
  157.7 0.0 collective-permute-done.15
  157.7 1.1 constant_dynamic-update-slice_fusion.1
  158.9 0.0 copy-start
  159.0 0.0 copy-start.1
  159.0 0.3 collective-permute-start.16
  159.3 4.2 %leaf_backward.2 = (bf16[32,128,256]{2,1,0:T(8,128)(2,1)S(1)}, bf16[32,128,128]{2,1,0:T(8,128)(2,1)S(1)}, bf16[32,5,128,128]{3,2,1,0:T(8,128)(2,1)S(1)}, bf16[1,128,256]{2,1,0:T(8,128)(2,1)}) custom-call(s32[1,32]{1,0:T(1,128)} %order_ref.1, bf16[8,128,256]{2,1,0:T(8,128)(2,1)} %copy-done.2, bf16[32,128,256]{2,1,0:T(8,128)(2,1)} %get-tuple-element.61.refs_0_, ...), custom_call_target="tpu_custom_call" | custom-call | tf_op jit(solution)/shard_map/leaf_backward/pallas_call | solution.py:135
  163.5 5.2 %leaf_backward.3 = bf16[32,128,256]{2,1,0:T(8,128)(2,1)} custom-call(s32[5,32]{1,0:T(8,128)S(1)} %bitcast.15, s32[32]{0:T(128)S(1)} %copy-done.1, bf16[32,128,256]{2,1,0:T(8,128)(2,1)S(1)} %get-tuple-element.64.refs_2_, bf16[32,128,128]{2,1,0:T(8,128)(2,1)S(1)} %get-tuple-element.65.refs_3_, bf16[32,5,128,128]{3,2,1,0:T(8,128)(2,1)S(1)} %get-tuple-element.66.refs_4_, ...), custom_call_target="tpu_custom_call" | custom-call | tf_op jit(solution)/shard_map/leaf_backward/pallas_call | solution.py:191
  (31 shorter events, 0.2 us)
Async XLA Ops:
  9.1 2.0 %collective-permute-start = (bf16[8,128,256]{2,1,0:T(8,128)(2,1)S(1)}, bf16[8,128,256]{2,1,0:T(8,128)(2,1)S(1)}, u32[]{:S(2)}, u32[]{:S(2)}) collective-permute-start(bf16[8,128,256]{2,1,0:T(8,128)(2,1)S(1)} %get-tuple-element.36), channel_id=1, source_target_pairs={{0,32},{32,0},{64,96},{96,64},{128,160},{160,128},{192,224},{224,1... | collective-permute-start | bytes 1572872 | tf_op jit(solution)/shard_map/sum_terms/ppermute | solution.py:28
  11.1 10.2 %collective-permute-start.1 = (bf16[24,128,256]{2,1,0:T(8,128)(2,1)S(1)}, bf16[24,128,256]{2,1,0:T(8,128)(2,1)S(1)}, u32[]{:S(2)}, u32[]{:S(2)}) collective-permute-start(bf16[24,128,256]{2,1,0:T(8,128)(2,1)S(1)} %get-tuple-element.43), channel_id=1, source_target_pairs={{0,32},{32,0},{64,96},{96,64},{128,160},{160,128},{192,224},{224,1... | collective-permute-start | bytes 4718600 | tf_op jit(solution)/shard_map/sum_terms/ppermute | solution.py:28
  11.4 9.9 %collective-permute-start.2 = (bf16[4,128,256]{2,1,0:T(8,128)(2,1)S(1)}, bf16[4,128,256]{2,1,0:T(8,128)(2,1)S(1)}, u32[]{:S(2)}, u32[]{:S(2)}) collective-permute-start(bf16[4,128,256]{2,1,0:T(8,128)(2,1)S(1)} %get-tuple-element.73), channel_id=1, source_target_pairs={{0,1},{1,2},{2,3},{3,0},{4,5},{5,6},{6,7},{7,4},{8,9},{9,10},{10,1... | collective-permute-start | bytes 786440 | tf_op jit(solution)/shard_map/sum_terms/ppermute | solution.py:207
  13.0 8.3 %collective-permute-start.4 = (bf16[4,128,256]{2,1,0:T(8,128)(2,1)S(1)}, bf16[4,128,256]{2,1,0:T(8,128)(2,1)S(1)}, u32[]{:S(2)}, u32[]{:S(2)}) collective-permute-start(bf16[4,128,256]{2,1,0:T(8,128)(2,1)S(1)} %get-tuple-element.74), channel_id=1, source_target_pairs={{0,3},{1,0},{2,1},{3,2},{4,7},{5,4},{6,5},{7,6},{8,11},{9,8},{10,9... | collective-permute-start | bytes 786440 | tf_op jit(solution)/shard_map/sum_terms/ppermute | solution.py:207
  22.6 14.9 %collective-permute-start.3 = (bf16[8,128,256]{2,1,0:T(8,128)(2,1)}, bf16[8,128,256]{2,1,0:T(8,128)(2,1)}, u32[]{:S(2)}, u32[]{:S(2)}) collective-permute-start(bf16[8,128,256]{2,1,0:T(8,128)(2,1)} %get-tuple-element.71), channel_id=1, source_target_pairs={{0,1},{1,2},{2,3},{3,0},{4,5},{5,6},{6,7},{7,4},{8,9},{9,10},{10,1... | collective-permute-start | bytes 1572872 | tf_op jit(solution)/shard_map/sum_terms/ppermute | solution.py:207
  24.1 13.4 %collective-permute-start.5 = (bf16[8,128,256]{2,1,0:T(8,128)(2,1)}, bf16[8,128,256]{2,1,0:T(8,128)(2,1)}, u32[]{:S(2)}, u32[]{:S(2)}) collective-permute-start(bf16[8,128,256]{2,1,0:T(8,128)(2,1)} %get-tuple-element.72), channel_id=1, source_target_pairs={{0,3},{1,0},{2,1},{3,2},{4,7},{5,4},{6,5},{7,6},{8,11},{9,8},{10,9... | collective-permute-start | bytes 1572872 | tf_op jit(solution)/shard_map/sum_terms/ppermute | solution.py:207
  28.4 20.9 %copy-start.12 = (bf16[128,1024]{1,0:T(8,128)(2,1)S(1)}, bf16[128,1024]{1,0:T(8,128)(2,1)}, u32[]{:S(2)}) copy-start(bf16[128,1024]{1,0:T(8,128)(2,1)} %get-tuple-element.49) | copy-start | bytes 786436
  28.4 36.3 %copy-start.9 = (bf16[1,128,256]{2,1,0:T(8,128)(2,1)S(1)}, bf16[1,128,256]{2,1,0:T(8,128)(2,1)}, u32[]{:S(2)}) copy-start(bf16[1,128,256]{2,1,0:T(8,128)(2,1)} %param.13) | copy-start | bytes 196612
  39.8 29.3 %copy-start.11 = (bf16[128,1024]{1,0:T(8,128)(2,1)S(1)}, bf16[128,1024]{1,0:T(8,128)(2,1)}, u32[]{:S(2)}) copy-start(bf16[128,1024]{1,0:T(8,128)(2,1)} %get-tuple-element.52) | copy-start | bytes 786436
  39.8 24.9 %all-to-all-start = ((bf16[8,128,256]{2,1,0:T(8,128)(2,1)}), bf16[8,128,256]{2,1,0:T(8,128)(2,1)S(1)}, u32[]{:S(2)}, u32[]{:S(2)}) async-start(bf16[8,128,256]{2,1,0:T(8,128)(2,1)} %add_convert_fusion), calls=%async_computation | async-start | bytes 1048576 | tf_op jit(solution)/shard_map/sum_terms/all_to_all | solution.py:23
  48.4 8.0 %collective-permute-start.6 = (bf16[128,1024]{1,0:T(8,128)(2,1)}, bf16[128,1024]{1,0:T(8,128)(2,1)S(1)}, u32[]{:S(2)}, u32[]{:S(2)}) collective-permute-start(bf16[128,1024]{1,0:T(8,128)(2,1)} %get-tuple-element.47), channel_id=1, source_target_pairs={{0,1},{1,2},{2,3},{3,0},{4,5},{5,6},{6,7},{7,4},{8,9},{9,10},{10,1... | collective-permute-start | bytes 786440 | tf_op jit(solution)/shard_map/spread_panels/ppermute | solution.py:207
  49.3 7.1 %collective-permute-start.7 = (bf16[128,1024]{1,0:T(8,128)(2,1)S(1)}, bf16[128,1024]{1,0:T(8,128)(2,1)S(1)}, u32[]{:S(2)}, u32[]{:S(2)}) collective-permute-start(bf16[128,1024]{1,0:T(8,128)(2,1)S(1)} %copy-done.12), channel_id=1, source_target_pairs={{0,3},{1,0},{2,1},{3,2},{4,7},{5,4},{6,5},{7,6},{8,11},{9,8},{10,9... | collective-permute-start | bytes 786440 | tf_op jit(solution)/shard_map/spread_panels/ppermute | solution.py:207
  56.4 20.7 %copy-start.6 = (bf16[128,1024]{1,0:T(8,128)(2,1)}, bf16[128,1024]{1,0:T(8,128)(2,1)S(1)}, u32[]{:S(2)}) copy-start(bf16[128,1024]{1,0:T(8,128)(2,1)S(1)} %collective-permute-done.6.p1) | copy-start | bytes 786436
  56.4 20.7 %copy-start.7 = (bf16[128,1024]{1,0:T(8,128)(2,1)}, bf16[128,1024]{1,0:T(8,128)(2,1)S(1)}, u32[]{:S(2)}) copy-start(bf16[128,1024]{1,0:T(8,128)(2,1)S(1)} %collective-permute-done.7.p3) | copy-start | bytes 786436
  65.6 19.0 %all-to-all-start.1 = ((bf16[8,128,256]{2,1,0:T(8,128)(2,1)}), bf16[8,128,256]{2,1,0:T(8,128)(2,1)S(1)}, u32[]{:S(2)}, u32[]{:S(2)}) async-start(bf16[8,128,256]{2,1,0:T(8,128)(2,1)} %broadcast_in_dim.43), calls=%async_computation.1 | async-start | bytes 1048576 | tf_op jit(solution)/shard_map/separators/all_to_all | solution.py:23
  69.1 8.0 %collective-permute-start.8 = (bf16[128,1024]{1,0:T(8,128)(2,1)S(1)}, bf16[128,1024]{1,0:T(8,128)(2,1)S(1)}, u32[]{:S(2)}, u32[]{:S(2)}) collective-permute-start(bf16[128,1024]{1,0:T(8,128)(2,1)S(1)} %copy-done.11), channel_id=1, source_target_pairs={{0,2},{1,3},{2,0},{3,1},{4,6},{5,7},{6,4},{7,5},{8,10},{9,11},{10,... | collective-permute-start | bytes 786440 | tf_op jit(solution)/shard_map/spread_panels/ppermute | solution.py:207
  77.1 0.7 copy-start.8
  80.0 18.2 %copy-start.5 = (bf16[512,1024]{1,0:T(8,128)(2,1)S(1)}, bf16[512,1024]{1,0:T(8,128)(2,1)}, u32[]{:S(2)}) copy-start(bf16[512,1024]{1,0:T(8,128)(2,1)} %spread_panels.3) | copy-start | bytes 3145732
  86.2 9.0 %collective-permute-start.10 = (bf16[512,256]{1,0:T(8,128)(2,1)S(1)}, bf16[512,256]{1,0:T(8,128)(2,1)S(1)}, u32[]{:S(2)}, u32[]{:S(2)}) collective-permute-start(bf16[512,256]{1,0:T(8,128)(2,1)S(1)} %convolution_convert_fusion.1), channel_id=1, source_target_pairs={{0,1},{1,2},{2,3},{3,0},{4,5},{5,6},{6,7},{7,4},{8,9},{9,10},{10,1... | collective-permute-start | bytes 786440 | tf_op jit(solution)/shard_map/separators/ppermute | solution.py:207
  86.3 10.9 %collective-permute-start.11 = (bf16[512,256]{1,0:T(8,128)(2,1)S(1)}, bf16[512,256]{1,0:T(8,128)(2,1)S(1)}, u32[]{:S(2)}, u32[]{:S(2)}) collective-permute-start(bf16[512,256]{1,0:T(8,128)(2,1)S(1)} %convolution_convert_fusion.1), channel_id=1, source_target_pairs={{0,3},{1,0},{2,1},{3,2},{4,7},{5,4},{6,5},{7,6},{8,11},{9,8},{10,9... | collective-permute-start | bytes 786440 | tf_op jit(solution)/shard_map/separators/ppermute | solution.py:207
  89.5 8.5 %collective-permute-start.9 = (bf16[512,256]{1,0:T(8,128)(2,1)S(1)}, bf16[512,256]{1,0:T(8,128)(2,1)S(1)}, u32[]{:S(2)}, u32[]{:S(2)}) collective-permute-start(bf16[512,256]{1,0:T(8,128)(2,1)S(1)} %convolution_convert_fusion.1), channel_id=1, source_target_pairs={{0,2},{1,3},{2,0},{3,1},{4,6},{5,7},{6,4},{7,5},{8,10},{9,11},{10,... | collective-permute-start | bytes 786440 | tf_op jit(solution)/shard_map/separators/ppermute | solution.py:207
  98.7 21.4 %copy-start.10 = (s32[1,32]{1,0:T(1,128)S(1)}, s32[1,32]{1,0:T(1,128)}, u32[]{:S(2)}) copy-start(s32[1,32]{1,0:T(1,128)} %order_ref.1) | copy-start | bytes 388
  116.5 16.7 %all-to-all-start.3 = ((bf16[8,128,256]{2,1,0:T(8,128)(2,1)}), bf16[8,128,256]{2,1,0:T(8,128)(2,1)S(1)}, u32[]{:S(2)}, u32[]{:S(2)}) async-start(bf16[8,128,256]{2,1,0:T(8,128)(2,1)} %broadcast_in_dim.45), calls=%async_computation.3 | async-start | bytes 1048576 | tf_op jit(solution)/shard_map/spread_solution/all_to_all | solution.py:23
  133.2 24.5 %all-to-all-start.4 = ((bf16[8,128,256]{2,1,0:T(8,128)(2,1)}), bf16[8,128,256]{2,1,0:T(8,128)(2,1)S(1)}, u32[]{:S(2)}, u32[]{:S(2)}) async-start(bf16[8,128,256]{2,1,0:T(8,128)(2,1)} %select_reduce_fusion), calls=%async_computation.4 | async-start | bytes 1048576 | tf_op jit(solution)/shard_map/order_rows/all_to_all | solution.py:23
  136.7 13.3 %collective-permute-start.12 = (bf16[8,128,256]{2,1,0:T(8,128)(2,1)S(1)}, bf16[8,128,256]{2,1,0:T(8,128)(2,1)S(1)}, u32[]{:S(2)}, u32[]{:S(2)}) collective-permute-start(bf16[8,128,256]{2,1,0:T(8,128)(2,1)S(1)} %all-to-all-done.3), channel_id=1, source_target_pairs={{0,1},{1,2},{2,3},{3,0},{4,5},{5,6},{6,7},{7,4},{8,9},{9,10},{10,1... | collective-permute-start | bytes 1572872 | tf_op jit(solution)/shard_map/spread_solution/ppermute | solution.py:207
  137.8 12.4 %collective-permute-start.14 = (bf16[8,128,256]{2,1,0:T(8,128)(2,1)S(1)}, bf16[8,128,256]{2,1,0:T(8,128)(2,1)S(1)}, u32[]{:S(2)}, u32[]{:S(2)}) collective-permute-start(bf16[8,128,256]{2,1,0:T(8,128)(2,1)S(1)} %all-to-all-done.3), channel_id=1, source_target_pairs={{0,3},{1,0},{2,1},{3,2},{4,7},{5,4},{6,5},{7,6},{8,11},{9,8},{10,9... | collective-permute-start | bytes 1572872 | tf_op jit(solution)/shard_map/spread_solution/ppermute | solution.py:207
  150.0 0.8 copy-start.3
  150.0 7.7 %collective-permute-start.13 = (bf16[4,128,256]{2,1,0:T(8,128)(2,1)S(1)}, bf16[4,128,256]{2,1,0:T(8,128)(2,1)S(1)}, u32[]{:S(2)}, u32[]{:S(2)}) collective-permute-start(bf16[4,128,256]{2,1,0:T(8,128)(2,1)S(1)} %slice.51), channel_id=1, source_target_pairs={{0,1},{1,2},{2,3},{3,0},{4,5},{5,6},{6,7},{7,4},{8,9},{9,10},{10,1... | collective-permute-start | bytes 786440 | tf_op jit(solution)/shard_map/spread_solution/ppermute | solution.py:207
  150.8 6.9 %collective-permute-start.15 = (bf16[4,128,256]{2,1,0:T(8,128)(2,1)S(1)}, bf16[4,128,256]{2,1,0:T(8,128)(2,1)}, u32[]{:S(2)}, u32[]{:S(2)}) collective-permute-start(bf16[4,128,256]{2,1,0:T(8,128)(2,1)S(1)} %slice.52), channel_id=1, source_target_pairs={{0,3},{1,0},{2,1},{3,2},{4,7},{5,4},{6,5},{7,6},{8,11},{9,8},{10,9... | collective-permute-start | bytes 786440 | tf_op jit(solution)/shard_map/spread_solution/ppermute | solution.py:207
  153.5 5.4 %copy-start.4 = (bf16[8,128,256]{2,1,0:T(8,128)(2,1)S(1)}, bf16[8,128,256]{2,1,0:T(8,128)(2,1)}, u32[]{:S(2)}) copy-start(bf16[8,128,256]{2,1,0:T(8,128)(2,1)} %copy-done.3) | copy-start | bytes 1572868
  157.7 1.6 copy-start.2
  158.9 4.6 %copy-start = (s32[32,5]{0,1:T(8,128)S(1)}, s32[32,5]{0,1:T(8,128)}, u32[]{:S(2)}) copy-start(s32[32,5]{0,1:T(8,128)} %param.11) | copy-start | bytes 1924
  159.0 4.6 %copy-start.1 = (s32[32]{0:T(128)S(1)}, s32[32]{0:T(128)}, u32[]{:S(2)}) copy-start(s32[32]{0:T(128)} %refs_1_.2) | copy-start | bytes 388
  159.0 4.6 %collective-permute-start.16 = (bf16[32,128,256]{2,1,0:T(8,128)(2,1)S(1)}, bf16[32,128,256]{2,1,0:T(8,128)(2,1)S(1)}, u32[]{:S(2)}, u32[]{:S(2)}) collective-permute-start(bf16[32,128,256]{2,1,0:T(8,128)(2,1)S(1)} %constant_dynamic-update-slice_fusion.refs_5_), channel_id=1, source_target_pairs={{0,32},{32,0},{64,96},{96,64},{128,160},{160,128},{192,224},{224,1... | collective-permute-start | bytes 6291464 | tf_op jit(solution)/shard_map/leaf_backward/ppermute | solution.py:28
